TPU v7x, 256 devices: a whole 4x4x8 slice. The times are simulated.
256 devices in a mesh: ta: 8 (over x, core), af: 32 (over y, z).
Axes of the slice: x: 4, y: 4, z: 8, core: 2. Of those that a mesh axis runs over, the one named last changes fastest.
Arguments:
- features: bfloat16 [16, 16384, 384], P('ta', 'af'), may hold values from -6 to 6
- spatial_weights: bfloat16 [384, 1152], replicated
- spatial_output: bfloat16 [384, 384], replicated, may hold values from -0.3125 to 0.3125
- temporal_weights: bfloat16 [384, 1152], replicated
- temporal_output: bfloat16 [384, 384], replicated, may hold values from -0.3125 to 0.3125
- spatial_gain: float32 [384], replicated, may hold values from 0.1 to 1.9
- temporal_gain: float32 [384], replicated, may hold values from 0.1 to 1.9
- neighbours: int32 [128, 5], P('af'), may hold values from 0 to 127, as said below
- degrees: int32 [128], P('af'), may hold values from 2 to 5, as said below
- cotangent: bfloat16 [16, 16384, 384], P('ta', 'af'), may hold values from -6 to 6
Outputs:
- layer_output: bfloat16 [16, 16384, 384], P('ta', 'af')
- output_gradient: float32 [384, 384], P('af')
Inputs may be any that keep to these rules, and one draw needn't show every extreme that they name: `neighbours`: row b lists b first, then the other node blocks that block b attends to, all distinct, within 2 blocks of b, and always including b - 1 and b + 1 where they exist; slots from degrees[b] on repeat b. degrees[b] counts the listed blocks of row b; some block has 5 and some has 2.
All inputs are finite; a program needn't handle non-finite values.
Results may differ from a plain program's by a relative error of at most 0.028.
Values may be sent and summed in bfloat16 or wider, within the bound.
A program may use at most 128 MiB of HBM per device.

v0:
```python
import jax
import jax.numpy as jnp
from jax import lax
from jax.sharding import PartitionSpec as P

HEADS = 6
WIN = 12


def with_halo(cells, sides, width):
    for axis, dim in sides:
        count = lax.axis_size(axis)
        ends = count - 1
        head = lax.slice_in_dim(cells, 0, width, axis=dim)
        tail = lax.slice_in_dim(cells, cells.shape[dim] - width, cells.shape[dim], axis=dim)
        cells = jnp.concatenate(
            [
                lax.ppermute(tail, axis, [(i, (i + 1) % count) for i in range(ends)]),
                cells,
                lax.ppermute(head, axis, [((i + 1) % count, i) for i in range(ends)]),
            ],
            axis=dim,
        )
    return cells


def normed(inputs, gain):
    widened = inputs.astype(jnp.float32)
    mean_square = jnp.mean(widened * widened, axis=-1, keepdims=True)
    return (widened * lax.rsqrt(mean_square + 1e-06) * gain).astype(jnp.bfloat16)


def soft_weights(scores, allowed):
    masked = jnp.where(allowed, scores, -1e30)
    largest = jnp.max(masked, axis=-1, keepdims=True)
    powers = jnp.where(allowed, jnp.exp(masked - largest), 0.0)
    return (powers / jnp.sum(powers, axis=-1, keepdims=True)).astype(jnp.bfloat16)


def shards(
    features,
    spatial_weights,
    spatial_output,
    temporal_weights,
    temporal_output,
    spatial_gain,
    temporal_gain,
    neighbours,
    degrees,
    cotangent,
):
    hours_dev, nodes_dev, width = features.shape
    blocks_dev, slots = neighbours.shape
    block = nodes_dev // blocks_dev
    rim_blocks = 2
    rim = rim_blocks * block
    head_dim = width // HEADS
    scale = head_dim ** (-0.5)
    normed_spatial = normed(features, spatial_gain)
    flat_rows = normed_spatial.reshape(-1, width)
    projected = jnp.dot(flat_rows, spatial_weights, preferred_element_type=jnp.float32)
    projected = projected.astype(jnp.bfloat16).reshape(
        hours_dev, normed_spatial.shape[1], 3 * width
    )
    queries = projected[..., :width]
    key_value = with_halo(projected[..., width:], (("af", 1),), rim)
    base_block = lax.axis_index("af") * blocks_dev
    local_index = neighbours - base_block + rim_blocks
    stacked = key_value.reshape(hours_dev, blocks_dev + 2 * rim_blocks, block, 2 * width)
    selected = stacked[:, local_index]
    selected = selected.reshape(hours_dev, blocks_dev, slots * block, 2, HEADS, head_dim)
    query_heads = queries.reshape(hours_dev, blocks_dev, block, HEADS, head_dim)
    scores = (
        jnp.einsum(
            "hbqnd,hbknd->hbnqk",
            query_heads,
            selected[:, :, :, 0],
            preferred_element_type=jnp.float32,
        )
        * scale
    )
    allowed = (jnp.arange(slots * block) // block)[None, :] < degrees[:, None]
    weights = soft_weights(scores, allowed[None, :, None, None, :])
    attended = jnp.einsum(
        "hbnqk,hbknd->hbqnd", weights, selected[:, :, :, 1], preferred_element_type=jnp.float32
    )
    attended = attended.astype(jnp.bfloat16).reshape(-1, width)
    mixed = jnp.dot(attended, spatial_output, preferred_element_type=jnp.float32)
    hidden = (features.reshape(-1, width).astype(jnp.float32) + mixed).astype(jnp.bfloat16)
    normed_temporal = normed(hidden.reshape(hours_dev, nodes_dev, width), temporal_gain)
    flat_temporal = normed_temporal.reshape(-1, width)
    projected_time = jnp.dot(flat_temporal, temporal_weights, preferred_element_type=jnp.float32)
    projected_time = projected_time.astype(jnp.bfloat16).reshape(
        normed_temporal.shape[0], normed_temporal.shape[1], 3 * width
    )
    projected_time = lax.all_to_all(projected_time, "ta", split_axis=1, concat_axis=0, tiled=True)
    hours_all, node_part = (projected_time.shape[0], projected_time.shape[1])
    split_heads = projected_time.reshape(hours_all, node_part, 3, HEADS, head_dim)
    scores_time = (
        jnp.einsum(
            "tnhd,snhd->nhts",
            split_heads[:, :, 0],
            split_heads[:, :, 1],
            preferred_element_type=jnp.float32,
        )
        * scale
    )
    hour_index = jnp.arange(hours_all)
    visible = (hour_index[None, :] <= hour_index[:, None]) & (
        hour_index[None, :] > hour_index[:, None] - WIN
    )
    weights_time = soft_weights(scores_time, visible)
    attended_time = jnp.einsum(
        "nhts,snhd->tnhd", weights_time, split_heads[:, :, 2], preferred_element_type=jnp.float32
    )
    attended_time = attended_time.astype(jnp.bfloat16).reshape(hours_all, node_part, width)
    returned = lax.all_to_all(attended_time, "ta", split_axis=0, concat_axis=1, tiled=True)
    flat_back = returned.reshape(-1, width)
    temporal_mixed = jnp.dot(flat_back, temporal_output, preferred_element_type=jnp.float32)
    layer_output = (
        (hidden.astype(jnp.float32) + temporal_mixed)
        .astype(jnp.bfloat16)
        .reshape(hours_dev, nodes_dev, width)
    )
    flat_cotangent = cotangent.reshape(-1, width)
    total_tokens = flat_back.shape[0] * lax.axis_size("ta") * lax.axis_size("af")
    grad_scale = total_tokens ** (-0.5)
    owned = lax.psum_scatter(
        (
            lax.dot_general(
                flat_back,
                flat_cotangent,
                (((0,), (0,)), ((), ())),
                preferred_element_type=jnp.float32,
            )
            * grad_scale
        ).astype(jnp.bfloat16),
        "af",
        scatter_dimension=0,
        tiled=True,
    ).astype(jnp.float32)
    gradient = lax.psum(owned, "ta")
    return (layer_output, gradient)


def solution(mesh):
    return jax.shard_map(
        shards,
        mesh=mesh,
        in_specs=(
            P("ta", "af", None),
            P(),
            P(),
            P(),
            P(),
            P(),
            P(),
            P("af", None),
            P("af"),
            P("ta", "af", None),
        ),
        out_specs=(P("ta", "af", None), P("af", None)),
        check_vma=False,
    )
```

profile of v0, /device:TPU:1, one launch (start us, length us, event | category | flops | bytes accessed | tf_op | source)
XLA Modules:
  0.0 329.8 jit_solution(8078194678099588255)
XLA Ops:
  0.6 0.0 copy-start
  0.6 1.4 multiply_reduce_fusion
  2.1 1.4 multiply_convert_fusion
  3.5 1.4 convolution_convert_fusion.1
  5.0 1.3 fusion.39
  6.2 5.4 %collective-permute-start = (bf16[2,256,768]{2,1,0:T(8,128)(2,1)}, bf16[2,256,768]{2,1,0:T(8,128)(2,1)}, u32[]{:S(2)}, u32[]{:S(2)}) collective-permute-start(bf16[2,256,768]{2,1,0:T(8,128)(2,1)} %get-tuple-element.5), channel_id=1, source_target_pairs={{0,1},{1,2},{2,3},{3,4},{4,5},{5,6},{6,7},{7,8},{8,9},{9,10},{10,1... | collective-permute-start | bytes 2359304 | tf_op jit(solution)/shard_map/ppermute | solution.py:18
  11.6 1.3 collective-permute-start.1
  12.9 0.1 slice.41
  13.0 0.0 copy-start.7
  13.0 0.1 slice.44
  13.2 0.1 reshape.133
  13.2 0.3 copy.69
  13.5 0.2 reshape.122
  13.8 0.1 broadcast_compare_fusion
  13.8 13.4 %collective-permute-done = bf16[2,256,768]{2,1,0:T(8,128)(2,1)} collective-permute-done((bf16[2,256,768]{2,1,0:T(8,128)(2,1)}, bf16[2,256,768]{2,1,0:T(8,128)(2,1)}, u32[]{:S(2)}, u32[]{:S(2)}) %collective-permute-start) | collective-permute-done | bytes 786464 | tf_op jit(solution)/shard_map/ppermute | solution.py:18
  27.2 4.7 %collective-permute-done.1 = bf16[2,256,768]{2,1,0:T(8,128)(2,1)} collective-permute-done((bf16[2,256,768]{2,1,0:T(8,128)(2,1)}, bf16[2,256,768]{2,1,0:T(8,128)(2,1)}, u32[]{:S(2)}, u32[]{:S(2)}) %collective-permute-start.1) | collective-permute-done | bytes 786464 | tf_op jit(solution)/shard_map/ppermute | solution.py:20
  31.9 2.9 pad_maximum_fusion
  34.8 7.2 %gather_fusion = bf16[20,2,128,768]{3,2,1,0:T(8,128)(2,1)} fusion(bf16[2,8,128,768]{3,2,1,0:T(8,128)(2,1)} %bitcast.70, s32[1024]{0:T(1024)S(1)} %pad_clamp_fusion), kind=kCustom, calls=%fused_computation | custom fusion | bytes 15728720 | tf_op jit(solution)/shard_map/gather | solution.py:70
  42.0 15.7 %copy.52 = bf16[2,4,5,128,768]{3,2,4,1,0:T(8,128)(2,1)} copy(bf16[2,4,5,128,768]{4,3,0,2,1:T(8,128)(2,1)} %bitcast.71) | data formatting | bytes 15728640 | tf_op jit(solution)/shard_map/gather | solution.py:70
  57.6 18.4 %reshape.121 = bf16[2,4,640,2,6,64]{2,5,4,3,1,0:T(8,128)(2,1)} reshape(bf16[2,4,5,128,768]{3,2,4,1,0:T(8,128)(2,1)} %copy.52) | data formatting | bytes 15728640 | tf_op jit(solution)/shard_map/reshape | solution.py:71
  76.0 9.9 %fusion.8 = f32[2,4,6,128,640]{4,3,2,1,0:T(8,128)} fusion(bf16[2,4,640,2,6,64]{2,5,4,3,1,0:T(8,128)(2,1)} %reshape.121, bf16[2,4,128,6,64]{2,1,4,3,0:T(4,128)(2,1)S(1)} %reshape.122), kind=kOutput, calls=%fused_computation.12 | convolution fusion | flops 503316480 | bytes 20447232 | tf_op jit(solution)/shard_map/hbqnd,hbknd->hbnqk/dot_general | solution.py:74
  85.9 17.3 %fusion.40 = (f32[2,4,6,128]{3,2,1,0:T(8,128)S(1)}, f32[2,4,6,128,640]{4,3,2,1,0:T(8,128)}) fusion(f32[2,4,6,128,640]{4,3,2,1,0:T(8,128)} %fusion.8, pred[4,640]{1,0:T(4,128)(4,1)S(1)} %broadcast_compare_fusion), kind=kOutput, calls=%fused_computation.73 | output fusion | flops 27525760 | bytes 31484416 | tf_op jit(solution)/shard_map/sub | solution.py:36
  103.2 9.9 %fusion.20 = bf16[2,4,128,6,64]{2,4,3,1,0:T(8,128)(2,1)S(1)} fusion(f32[2,4,6,128,640]{4,3,2,1,0:T(8,128)} %get-tuple-element.8, f32[2,4,6,128]{3,2,1,0:T(8,128)S(1)} %get-tuple-element.7, bf16[2,4,640,2,6,64]{2,5,4,3,1,0:T(8,128)(2,1)} %reshape.121), kind=kOutput, calls=%fused_computation.38 | convolution fusion | flops 511574016 | bytes 20471808 | tf_op jit(solution)/shard_map/hbnqk,hbknd->hbqnd/dot_general | solution.py:84
  113.1 0.0 copy-start.11
  113.1 0.6 copy.57
  113.7 0.6 reshape.123
  114.3 1.8 fusion.9
  116.1 0.9 copy-done.3
  117.0 1.5 convolution_convert_fusion
  118.5 3.8 %copy.58 = bf16[2,512,1152]{2,0,1:T(2,128)(2,1)} copy(bf16[2,512,1152]{2,1,0:T(8,128)(2,1)S(1)} %bitcast.79) | data formatting | bytes 4718592 | tf_op jit(solution)/shard_map/reshape | solution.py:93
  122.4 6.2 %all-to-all-start = ((bf16[2,512,1152]{2,0,1:T(2,128)(2,1)}), bf16[2,512,1152]{2,0,1:T(2,128)(2,1)S(1)}, u32[]{:S(2)}, u32[]{:S(2)}) async-start(bf16[2,512,1152]{2,0,1:T(2,128)(2,1)} %copy.58), calls=%async_computation | async-start | bytes 4718592 | tf_op jit(solution)/shard_map/all_to_all | solution.py:96
  128.5 0.1 fusion.30
  128.6 29.1 %all-to-all-done = bf16[2,512,1152]{2,0,1:T(2,128)(2,1)S(1)} async-done(((bf16[2,512,1152]{2,0,1:T(2,128)(2,1)}), bf16[2,512,1152]{2,0,1:T(2,128)(2,1)S(1)}, u32[]{:S(2)}, u32[]{:S(2)}) %all-to-all-start) | async-done | bytes 2359328 | tf_op jit(solution)/shard_map/all_to_all | solution.py:96
  157.7 0.3 copy.59
  158.0 0.2 copy.60
  158.2 5.8 %reshape.125 = bf16[16,64,3,6,64]{4,3,2,1,0:T(8,128)(2,1)} reshape(bf16[8,2,64,1152]{3,2,1,0:T(8,128)(2,1)S(1)} %copy.60) | data formatting | bytes 4718592 | tf_op jit(solution)/shard_map/reshape | solution.py:98
  164.0 4.5 %fusion.38 = (bf16[16,64,1,6,64]{4,3,2,1,0:T(8,128)(2,1)S(1)}, bf16[16,64,1,6,64]{4,3,2,1,0:T(8,128)(2,1)S(1)}, bf16[16,64,1,6,64]{4,3,2,1,0:T(8,128)(2,1)S(1)}) fusion(bf16[16,64,3,6,64]{4,3,2,1,0:T(8,128)(2,1)} %reshape.125), kind=kLoop, calls=%fused_computation.71 | loop fusion | bytes 4718592 | tf_op jit(solution)/shard_map/slice | solution.py:114
  168.5 3.6 %fusion.13 = f32[64,6,16,16]{2,3,1,0:T(8,128)} fusion(bf16[16,64,1,6,64]{4,3,2,1,0:T(8,128)(2,1)S(1)} %get-tuple-element.3, bf16[16,64,1,6,64]{4,3,2,1,0:T(8,128)(2,1)S(1)} %get-tuple-element.4), kind=kOutput, calls=%fused_computation.27 | convolution fusion | flops 12582912 | bytes 1966080 | tf_op jit(solution)/shard_map/tnhd,snhd->nhts/dot_general | solution.py:100
  172.1 2.8 copy.64
  174.9 2.0 fusion.41
  176.8 0.1 divide_convert_fusion.6
  176.9 2.1 copy.65
  179.0 2.6 fusion.15
  181.6 0.5 copy.66
  182.1 1.2 reshape.126
  183.4 0.0 copy-start.10
  183.4 0.0 copy-start.8
  183.4 0.0 copy-start.4
  183.4 15.6 %all_to_all.30 = bf16[16,64,384]{2,1,0:T(8,128)(2,1)S(1)} all-to-all(bf16[16,64,384]{2,1,0:T(8,128)(2,1)S(1)} %reshape.126), channel_id=1, replica_groups=mesh['ta'=8,'af'=32] {'ta'}, dimensions={0} | all-to-all | bytes 1572864 | tf_op jit(solution)/shard_map/all_to_all | solution.py:117
  199.0 0.1 copy.67
  199.1 0.6 fusion.21
  199.7 64.9 %fusion = bf16[16,384]{1,0:T(8,128)(2,1)S(1)} fusion(bf16[384,384]{1,0:T(8,128)(2,1)S(1)} %fusion.21), kind=kCustom, calls=%all-reduce-scatter | all-reduce-scatter fusion | flops 196609 | bytes 308224
  264.7 1.3 collective-permute-start.2
  266.0 1.3 collective-permute-start.3
  267.3 1.3 collective-permute-start.9
  268.6 0.6 dynamic-slice.4
  269.8 1.3 collective-permute-start.4
  271.1 1.3 collective-permute-start.5
  272.4 3.2 collective-permute-start.6
  275.6 10.9 %collective-permute-start.7 = (bf16[16,384]{1,0:T(8,128)(2,1)S(1)}, bf16[16,384]{1,0:T(8,128)(2,1)S(1)}, u32[]{:S(2)}, u32[]{:S(2)}) collective-permute-start(bf16[16,384]{1,0:T(8,128)(2,1)S(1)} %fusion), channel_id=1, source_target_pairs={{0,6},{1,7},{2,8},{3,9},{4,10},{5,11},{6,12},{7,13},{8,14},{9,15},... | collective-permute-start | bytes 36872
  286.5 3.1 collective-permute-start.8
  289.7 1.5 fusion.12
  291.2 1.2 concatenate.4
  292.5 37.3 %psum.7 = f32[12,384]{1,0:T(8,128)} all-reduce(f32[12,384]{1,0:T(8,128)S(1)} %dynamic-slice_convert_fusion), channel_id=1, replica_groups=mesh['ta'=8,'af'=32] {'ta'}, use_global_device_ids=true, to_apply=%region_7.8 | all-reduce | flops 4608 | bytes 36864 | tf_op jit(solution)/shard_map/psum | solution.py:142
  (33 shorter events, 0.1 us)
Async XLA Ops:
  0.6 2.9 copy-start
  6.2 6.9 %copy-start.6 = (s32[4,5]{1,0:T(4,128)S(1)}, s32[4,5]{1,0:T(4,128)}, u32[]{:S(2)}) copy-start(s32[4,5]{1,0:T(4,128)} %param.17) | copy-start | bytes 244
  6.2 21.0 %collective-permute-start = (bf16[2,256,768]{2,1,0:T(8,128)(2,1)}, bf16[2,256,768]{2,1,0:T(8,128)(2,1)}, u32[]{:S(2)}, u32[]{:S(2)}) collective-permute-start(bf16[2,256,768]{2,1,0:T(8,128)(2,1)} %get-tuple-element.5), channel_id=1, source_target_pairs={{0,1},{1,2},{2,3},{3,4},{4,5},{5,6},{6,7},{7,8},{8,9},{9,10},{10,1... | collective-permute-start | bytes 2359304 | tf_op jit(solution)/shard_map/ppermute | solution.py:18
  11.6 20.3 %collective-permute-start.1 = (bf16[2,256,768]{2,1,0:T(8,128)(2,1)}, bf16[2,256,768]{2,1,0:T(8,128)(2,1)}, u32[]{:S(2)}, u32[]{:S(2)}) collective-permute-start(bf16[2,256,768]{2,1,0:T(8,128)(2,1)} %get-tuple-element.6), channel_id=1, source_target_pairs={{1,0},{2,1},{3,2},{4,3},{5,4},{6,5},{7,6},{8,7},{9,8},{10,9},{11,1... | collective-permute-start | bytes 2359304 | tf_op jit(solution)/shard_map/ppermute | solution.py:20
  13.0 0.7 copy-start.7
  113.1 1.2 copy-start.2
  113.1 3.9 %copy-start.9 = (bf16[384,1152]{1,0:T(8,128)(2,1)S(1)}, bf16[384,1152]{1,0:T(8,128)(2,1)}, u32[]{:S(2)}) copy-start(bf16[384,1152]{1,0:T(8,128)(2,1)} %param.13) | copy-start | bytes 2654212
  113.1 3.9 %copy-start.11 = (f32[384]{0:T(512)S(1)}, f32[384]{0:T(512)}, u32[]{:S(2)}) copy-start(f32[384]{0:T(512)} %param.16) | copy-start | bytes 4612
  116.1 0.9 copy-start.3
  122.4 35.3 %all-to-all-start = ((bf16[2,512,1152]{2,0,1:T(2,128)(2,1)}), bf16[2,512,1152]{2,0,1:T(2,128)(2,1)S(1)}, u32[]{:S(2)}, u32[]{:S(2)}) async-start(bf16[2,512,1152]{2,0,1:T(2,128)(2,1)} %copy.58), calls=%async_computation | async-start | bytes 4718592 | tf_op jit(solution)/shard_map/all_to_all | solution.py:96
  183.4 15.8 %copy-start.10 = (bf16[2,512,384]{2,1,0:T(8,128)(2,1)S(1)}, bf16[2,512,384]{2,1,0:T(8,128)(2,1)}, u32[]{:S(2)}) copy-start(bf16[2,512,384]{2,1,0:T(8,128)(2,1)} %param.19) | copy-start | bytes 2359300
  183.4 85.2 %copy-start.8 = (u32[256]{0:T(256)S(1)}, u32[256]{0:T(256)}, u32[]{:S(2)}) copy-start(u32[256]{0:T(256)} %constant.56) | copy-start | bytes 3076
  183.4 106.3 %copy-start.4 = (bf16[1024,384]{1,0:T(8,128)(2,1)S(1)}, bf16[1024,384]{1,0:T(8,128)(2,1)}, u32[]{:S(2)}) copy-start(bf16[1024,384]{1,0:T(8,128)(2,1)} %copy-done.3) | copy-start | bytes 2359300
  183.4 106.3 %copy-start.5 = (bf16[384,384]{1,0:T(8,128)(2,1)S(1)}, bf16[384,384]{1,0:T(8,128)(2,1)}, u32[]{:S(2)}) copy-start(bf16[384,384]{1,0:T(8,128)(2,1)} %param.14) | copy-start | bytes 884740
  199.0 130.8 %copy-start.1 = (bf16[384,1152]{1,0:T(8,128)(2,1)S(1)}, bf16[384,1152]{1,0:T(8,128)(2,1)}, u32[]{:S(2)}) copy-start(bf16[384,1152]{1,0:T(8,128)(2,1)} %param.11) | copy-start | bytes 2654212
  264.7 10.9 %collective-permute-start.2 = (bf16[16,384]{1,0:T(8,128)(2,1)S(1)}, bf16[16,384]{1,0:T(8,128)(2,1)S(1)}, u32[]{:S(2)}, u32[]{:S(2)}) collective-permute-start(bf16[16,384]{1,0:T(8,128)(2,1)S(1)} %fusion), channel_id=1, source_target_pairs={{0,1},{1,2},{2,3},{3,4},{4,5},{5,6},{6,7},{7,8},{8,9},{9,10},{10,1... | collective-permute-start | bytes 36872
  266.0 20.5 %collective-permute-start.3 = (bf16[16,384]{1,0:T(8,128)(2,1)S(1)}, bf16[16,384]{1,0:T(8,128)(2,1)S(1)}, u32[]{:S(2)}, u32[]{:S(2)}) collective-permute-start(bf16[16,384]{1,0:T(8,128)(2,1)S(1)} %fusion), channel_id=1, source_target_pairs={{0,2},{1,3},{2,4},{3,5},{4,6},{5,7},{6,8},{7,9},{8,10},{9,11},{10,... | collective-permute-start | bytes 36872
  267.3 5.1 %collective-permute-start.9 = (bf16[12,384]{1,0:T(8,128)(2,1)S(1)}, bf16[12,384]{1,0:T(8,128)(2,1)S(1)}, u32[]{:S(2)}, u32[]{:S(2)}) collective-permute-start(bf16[12,384]{1,0:T(8,128)(2,1)S(1)} %slice.49), channel_id=1, source_target_pairs={{0,8},{1,9},{2,10},{3,11},{4,12},{5,13},{6,14},{7,15},{8,16},{9,17... | collective-permute-start | bytes 27656
  269.8 21.4 %collective-permute-start.4 = (bf16[16,384]{1,0:T(8,128)(2,1)S(1)}, bf16[16,384]{1,0:T(8,128)(2,1)S(1)}, u32[]{:S(2)}, u32[]{:S(2)}) collective-permute-start(bf16[16,384]{1,0:T(8,128)(2,1)S(1)} %fusion), channel_id=1, source_target_pairs={{0,3},{1,4},{2,5},{3,6},{4,7},{5,8},{6,9},{7,10},{8,11},{9,12},{10... | collective-permute-start | bytes 36872
  271.1 20.1 %collective-permute-start.5 = (bf16[16,384]{1,0:T(8,128)(2,1)S(1)}, bf16[16,384]{1,0:T(8,128)(2,1)S(1)}, u32[]{:S(2)}, u32[]{:S(2)}) collective-permute-start(bf16[16,384]{1,0:T(8,128)(2,1)S(1)} %fusion), channel_id=1, source_target_pairs={{0,4},{1,5},{2,6},{3,7},{4,8},{5,9},{6,10},{7,11},{8,12},{9,13},{1... | collective-permute-start | bytes 36872
  272.4 18.8 %collective-permute-start.6 = (bf16[16,384]{1,0:T(8,128)(2,1)S(1)}, bf16[16,384]{1,0:T(8,128)(2,1)S(1)}, u32[]{:S(2)}, u32[]{:S(2)}) collective-permute-start(bf16[16,384]{1,0:T(8,128)(2,1)S(1)} %fusion), channel_id=1, source_target_pairs={{0,5},{1,6},{2,7},{3,8},{4,9},{5,10},{6,11},{7,12},{8,13},{9,14},{... | collective-permute-start | bytes 36872
  275.6 15.6 %collective-permute-start.7 = (bf16[16,384]{1,0:T(8,128)(2,1)S(1)}, bf16[16,384]{1,0:T(8,128)(2,1)S(1)}, u32[]{:S(2)}, u32[]{:S(2)}) collective-permute-start(bf16[16,384]{1,0:T(8,128)(2,1)S(1)} %fusion), channel_id=1, source_target_pairs={{0,6},{1,7},{2,8},{3,9},{4,10},{5,11},{6,12},{7,13},{8,14},{9,15},... | collective-permute-start | bytes 36872
  286.5 4.7 %collective-permute-start.8 = (bf16[16,384]{1,0:T(8,128)(2,1)S(1)}, bf16[16,384]{1,0:T(8,128)(2,1)S(1)}, u32[]{:S(2)}, u32[]{:S(2)}) collective-permute-start(bf16[16,384]{1,0:T(8,128)(2,1)S(1)} %fusion), channel_id=1, source_target_pairs={{0,7},{1,8},{2,9},{3,10},{4,11},{5,12},{6,13},{7,14},{8,15},{9,16}... | collective-permute-start | bytes 36872
where the time goes:
time: 335 us; the launch traced here: 330 us
  blocking collectives  118 us (35%)
  local copies, waits for them, and re-layouts  68.5 us (20%)
  waiting for transfers between devices  47.2 us (14%)
  starting transfers between devices  36.5 us (11%)
  matrix products  32.8 us (10%)
  other arithmetic  25.2 us (8%)
    unnamed x1, blocking collectives  64.9 us
    psum x1, blocking collectives, shards(): gradient = lax.psum(owned, 'ta')  37.3 us
    all_to_all x1, waiting for transfers between devices, shards(): lax.all_to_all(projected_time, 'ta', split_axis=1, concat_axis=0, tiled=T...  29.1 us
    unnamed x8, starting transfers between devices  23.6 us
    gather x2, local copies, waits for them, and re-layouts, shards(): selected = stacked[:, local_index]  22.8 us
    sub x2, other arithmetic, soft_weights(): powers = jnp.where(allowed, jnp.exp(masked - largest), 0.0)  19.2 us
    reshape x1, local copies, waits for them, and re-layouts, shards(): selected.reshape(hours_dev, blocks_dev, slots * block, 2, HEADS, head_dim)  18.4 us
    all_to_all x1, blocking collectives, shards(): lax.all_to_all(attended_time, 'ta', split_axis=0, concat_axis=1, tiled=True)  15.6 us
  transfers between devices with their start and end apart: 11, of which 3 were waited for; matrix products, arithmetic and copies ran while one was open for 1% of the time, Pallas kernels for 0%

commit v1 on v0

v1 whole, which is shorter than its diff:
```python
import functools

import jax
import jax.numpy as jnp
from jax import lax
from jax.experimental import pallas as pl
from jax.experimental.pallas import tpu as pltpu
from jax.sharding import PartitionSpec as P

MESH = pl.DeviceIdType.MESH
F32 = jnp.float32
BF16 = jnp.bfloat16

WIDTH = 384
PAIRS = 3
BLOCK = 128
RIM = 256
SPAN = 640
WIN = 12
GROUP = 16
OWNED = 12
PADDED = 16
EXCLUDED = 1e30
SCORE_SCALE = 0.125 * 1.4426950408889634


def dot(a, b):
    return jnp.dot(a, b, preferred_element_type=F32)


def dot_nt(a, b):
    return lax.dot_general(a, b, (((1,), (1,)), ((), ())), preferred_element_type=F32)


def normed(rows, gain):
    mean_square = jnp.mean(rows * rows, axis=-1, keepdims=True)
    return (rows * lax.rsqrt(mean_square + 1e-06) * gain).astype(BF16)


def kernel(
    n_ta,
    n_af,
    tokens,
    x_ref,
    ws_ref,
    wso_ref,
    wt_ref,
    wto_ref,
    gs_ref,
    gt_ref,
    nb_ref,
    dg_ref,
    cot_ref,
    out_ref,
    grad_ref,
    halo,
    k_ext,
    q_diag,
    v_ext,
    ws_t,
    wt_t,
    staged,
    h_all,
    c_all,
    bias,
    out_staged,
    g_total,
    g_send,
    g_recv,
    t_send,
    t_recv,
    halo_send,
    halo_recv,
    c_send,
    c_recv,
    h_send,
    h_recv,
    o_send,
    o_recv,
    gs_sem,
    gr_sem,
    ts_sem,
    tr_sem,
    own_sem,
):
    ta = lax.axis_index("ta")
    af = lax.axis_index("af")
    hours_dev, nodes_dev, _ = x_ref.shape
    part = nodes_dev // n_ta
    blocks_dev = nodes_dev // BLOCK
    hours = hours_dev * n_ta
    groups = part // GROUP
    right = lax.rem(af + 1, n_af)
    left = lax.rem(af + n_af - 1, n_af)

    def to(ta_id, af_id, src, dst, send, recv):
        return pltpu.make_async_remote_copy(
            src_ref=src,
            dst_ref=dst,
            send_sem=send,
            recv_sem=recv,
            device_id=(ta_id, af_id),
            device_id_type=MESH,
        )

    def halo_right(h):
        return to(ta, right, x_ref.at[h, pl.ds(nodes_dev - RIM, RIM)], halo.at[h, 0], halo_send.at[h, 0], halo_recv.at[h, 0])

    def halo_left(h):
        return to(ta, left, x_ref.at[h, pl.ds(0, RIM)], halo.at[h, 1], halo_send.at[h, 1], halo_recv.at[h, 1])

    def cot_copy(peer, slot):
        rows = pl.ds(pl.multiple_of(peer * part, part), part)
        return to(peer, af, cot_ref.at[:, rows], c_all.at[pl.ds(slot * hours_dev, hours_dev)], c_send.at[peer], c_recv.at[slot])

    def hidden_copy(peer, h, slot):
        rows = pl.ds(pl.multiple_of(peer * part, part), part)
        return to(peer, af, staged.at[h, rows], h_all.at[slot * hours_dev + h], h_send.at[h, peer], h_recv.at[h, slot])

    def out_copy(g, peer, slot):
        rows = pl.ds(pl.multiple_of(g * GROUP, GROUP), GROUP)
        there = pl.ds(pl.multiple_of(slot * part + g * GROUP, GROUP), GROUP)
        src = out_staged.at[pl.ds(peer * hours_dev, hours_dev), rows]
        return to(peer, af, src, out_ref.at[:, there], o_send.at[g, peer], o_recv.at[g, slot])

    def grad_copy(peer, slot):
        return to(ta, peer, g_send.at[peer], g_recv.at[slot], gs_sem.at[peer], gr_sem.at[slot])

    def total_copy(peer, slot):
        return to(peer, af, t_send, t_recv.at[slot], ts_sem.at[peer], tr_sem.at[slot])

    def others(count, me, act):
        def step(i, carry):
            act(lax.rem(me + i, count))
            return carry

        lax.fori_loop(1, count, step, 0)

    barrier = pltpu.get_barrier_semaphore()
    others(n_ta, ta, lambda p: pl.semaphore_signal(barrier, inc=1, device_id=(p, af), device_id_type=MESH))
    others(n_af, af, lambda p: pl.semaphore_signal(barrier, inc=1, device_id=(ta, p), device_id_type=MESH))

    ws_t[0] = ws_ref[:, :WIDTH].T
    ws_t[1] = ws_ref[:, 2 * WIDTH :].T
    q_diag[...] = jnp.zeros_like(q_diag)
    v_ext[:, :, BLOCK:, :] = jnp.ones_like(v_ext[:, :, BLOCK:, :])

    pl.semaphore_wait(barrier, n_ta + n_af - 2)
    for h in range(hours_dev):
        halo_right(h).start()
        halo_left(h).start()
    others(n_ta, ta, lambda p: cot_copy(p, ta).start())
    own_cot = pltpu.make_async_copy(
        cot_ref.at[:, pl.ds(pl.multiple_of(ta * part, part), part)],
        c_all.at[pl.ds(ta * hours_dev, hours_dev)],
        own_sem.at[0],
    )
    own_cot.start()

    def keys_values(h, rows_normed, where):
        count = rows_normed.shape[0]
        k_ext[h, pl.ds(where, count), :] = dot(rows_normed, ws_ref[:, WIDTH : 2 * WIDTH]).astype(BF16)
        values = dot_nt(ws_t[1], rows_normed).astype(BF16)
        for pair in range(PAIRS):
            v_ext[h, pair, :BLOCK, pl.ds(where, count)] = values[pair * BLOCK : (pair + 1) * BLOCK]

    def own_rows(h, carry):
        rows = normed(x_ref[h].astype(F32), gs_ref[...])
        keys_values(h, rows, RIM)
        queries = (dot_nt(ws_t[0], rows) * SCORE_SCALE).astype(BF16)
        for pair in range(PAIRS):
            for b in range(blocks_dev):
                for k in range(2):
                    lo = k * (BLOCK // 2)
                    q_diag[h, pair, lo : lo + BLOCK // 2, (2 * b + k) * BLOCK : (2 * b + k + 1) * BLOCK] = queries[
                        pair * BLOCK + lo : pair * BLOCK + lo + BLOCK // 2, b * BLOCK : (b + 1) * BLOCK
                    ]
        return carry

    lax.fori_loop(0, hours_dev, own_rows, 0)

    wt_t[0] = wt_ref[:, :WIDTH].T
    wt_t[1] = wt_ref[:, 2 * WIDTH :].T
    key_index = lax.broadcasted_iota(jnp.int32, bias.shape, 0)
    query_index = lax.broadcasted_iota(jnp.int32, bias.shape, 1)
    ahead = query_index // GROUP - key_index // GROUP
    seen = (query_index % GROUP == key_index % GROUP) & (ahead >= 0) & (ahead < WIN)
    bias[...] = jnp.where(seen, 0.0, -EXCLUDED)
    g_total[...] = jnp.zeros_like(g_total)

    def spatial_block(h, i, carry):
        turn = jnp.where(i == 0, 2, jnp.where(i == 1, 1, jnp.where(i == 2, 3, 0)))
        b = lax.rem(ta // 2 + turn, blocks_dev)
        first = pl.multiple_of(b * BLOCK, BLOCK)
        penalty = []
        for o in range(5):
            listed = jnp.int32(0)
            for j in range(5):
                hit = (nb_ref[b, j] == af * blocks_dev + b + (o - 2)) & (j < dg_ref[b])
                listed = listed | hit.astype(jnp.int32)
            penalty.append((1 - listed).astype(F32) * EXCLUDED)
        attended = []
        for pair in range(PAIRS):
            columns = slice(pair * BLOCK, (pair + 1) * BLOCK)
            keys = k_ext[h, pl.ds(first, SPAN), columns]
            queries = q_diag[h, pair, :, pl.ds(pl.multiple_of(b * 2 * BLOCK, 2 * BLOCK), 2 * BLOCK)]
            scores = dot(keys, queries)
            tiles = [scores[o * BLOCK : (o + 1) * BLOCK] for o in range(5)]
            largest = None
            for tile, extra in zip(tiles, penalty, strict=True):
                here = jnp.max(tile, axis=0, keepdims=True) - extra
                largest = here if largest is None else jnp.maximum(largest, here)
            powers = [
                jnp.exp2(tile - (largest + extra)).astype(BF16)
                for tile, extra in zip(tiles, penalty, strict=True)
            ]
            summed = dot(v_ext[h, pair, :, pl.ds(first, SPAN)], jnp.concatenate(powers, axis=0))
            inverse = 1.0 / summed[BLOCK : BLOCK + 1]
            half = BLOCK // 2
            attended.append(summed[:half, :BLOCK] * inverse[:, :BLOCK])
            attended.append(summed[half:BLOCK, BLOCK:] * inverse[:, BLOCK:])
        attended = jnp.concatenate(attended, axis=0).T.astype(BF16)
        mixed = dot(attended, wso_ref[...])
        hidden = (x_ref[h, pl.ds(first, BLOCK)].astype(F32) + mixed).astype(BF16)
        staged[h, pl.ds(first, BLOCK)] = hidden
        for k in range(BLOCK // part):
            peer = b * (BLOCK // part) + k

            @pl.when(peer != ta)
            def _():
                hidden_copy(peer, h, ta).start()

            @pl.when(peer == ta)
            def _():
                h_all[ta * hours_dev + h] = hidden[k * part : (k + 1) * part]

        return carry

    def spatial_hour(h, carry):
        halo_right(h).wait_recv()
        halo_left(h).wait_recv()
        for side in range(2):
            rows = normed(halo[h, side].astype(F32), gs_ref[...])
            keys_values(h, rows, side * (RIM + nodes_dev))
        return lax.fori_loop(0, blocks_dev, functools.partial(spatial_block, h), carry)

    lax.fori_loop(0, hours_dev, spatial_hour, 0)

    own_cot.wait()
    others(n_ta, ta, lambda p: cot_copy(p, p).wait_recv())
    for h in range(hours_dev):
        others(n_ta, ta, lambda p, h=h: hidden_copy(p, h, p).wait_recv())

    tokens_group = hours * GROUP

    def temporal_group(g, carry):
        nodes = pl.ds(pl.multiple_of(g * GROUP, GROUP), GROUP)
        hidden = h_all[:, nodes].reshape(tokens_group, WIDTH).astype(F32)
        rows = normed(hidden, gt_ref[...])
        keys = dot(rows, wt_ref[:, WIDTH : 2 * WIDTH]).astype(BF16)
        queries = (dot_nt(wt_t[0], rows) * SCORE_SCALE).astype(BF16)
        values = dot_nt(wt_t[1], rows).astype(BF16)
        half = BLOCK // 2
        blank = jnp.zeros((half, tokens_group), BF16)
        ones = jnp.ones((PADDED, tokens_group), BF16)
        attended = []
        for head in range(2 * PAIRS):
            low = head * half
            mine = queries[low : low + half]
            padded = jnp.concatenate([mine, blank] if head % 2 == 0 else [blank, mine], axis=0)
            pair = slice(head // 2 * BLOCK, (head // 2 + 1) * BLOCK)
            scores = dot(keys[:, pair], padded) + bias[...]
            largest = jnp.max(scores, axis=0, keepdims=True)
            powers = jnp.exp2(scores - largest).astype(BF16)
            summed = dot(jnp.concatenate([values[low : low + half], ones], axis=0), powers)
            attended.append(summed[:half] * (1.0 / summed[half : half + 1]))
        attended = jnp.concatenate(attended, axis=0)
        cot = c_all[:, nodes].reshape(tokens_group, WIDTH)
        g_total[...] += dot(attended.astype(BF16), cot)
        mixed = dot(attended.T.astype(BF16), wto_ref[...])
        out_staged[:, nodes] = (hidden + mixed).astype(BF16).reshape(hours, GROUP, WIDTH)
        others(n_ta, ta, lambda p: out_copy(g, p, ta).start())
        return carry

    lax.fori_loop(0, groups, temporal_group, 0)
    own_out = pltpu.make_async_copy(
        out_staged.at[pl.ds(ta * hours_dev, hours_dev)],
        out_ref.at[:, pl.ds(pl.multiple_of(ta * part, part), part)],
        own_sem.at[1],
    )
    own_out.start()

    term = (g_total[...] * tokens ** (-0.5)).astype(BF16)
    slot = lax.broadcasted_iota(jnp.int32, (n_af * PADDED, WIDTH), 0)
    row = lax.broadcasted_iota(jnp.int32, (n_af * PADDED, WIDTH), 1)
    inside = slot % PADDED
    picks = (inside < OWNED) & (slot // PADDED * OWNED + inside == row)
    picks = jnp.where(picks, 1.0, 0.0).astype(BF16)
    g_send[...] = dot(picks, term).astype(BF16).reshape(n_af, PADDED, WIDTH)
    others(n_af, af, lambda p: grad_copy(p, af).start())
    g_recv[af] = g_send[af]
    others(n_af, af, lambda p: grad_copy(p, p).wait_recv())
    t_send[...] = jnp.sum(g_recv[...].astype(F32), axis=0)
    others(n_ta, ta, lambda p: total_copy(p, ta).start())
    t_recv[ta] = t_send[...]
    others(n_ta, ta, lambda p: total_copy(p, p).wait_recv())
    grad_ref[...] = jnp.sum(t_recv[...], axis=0)[:OWNED]

    def out_waits(g, carry):
        others(n_ta, ta, lambda p: out_copy(g, p, p).wait_recv())
        others(n_ta, ta, lambda p: out_copy(g, p, ta).wait_send())
        return carry

    lax.fori_loop(0, groups, out_waits, 0)
    own_out.wait()
    for h in range(hours_dev):
        halo_right(h).wait_send()
        halo_left(h).wait_send()
        others(n_ta, ta, lambda p, h=h: hidden_copy(p, h, ta).wait_send())
    others(n_ta, ta, lambda p: cot_copy(p, ta).wait_send())
    others(n_af, af, lambda p: grad_copy(p, af).wait_send())
    others(n_ta, ta, lambda p: total_copy(p, ta).wait_send())


def shards(n_ta, n_af, features, ws, wso, wt, wto, gain_s, gain_t, neighbours, degrees, cotangent):
    hours_dev, nodes_dev, width = features.shape
    part = nodes_dev // n_ta
    hours = hours_dev * n_ta
    groups = part // GROUP
    extended = nodes_dev + 2 * RIM
    vmem = pl.BlockSpec(memory_space=pltpu.VMEM)
    smem = pl.BlockSpec(memory_space=pltpu.SMEM)
    anywhere = pl.BlockSpec(memory_space=pl.ANY)
    dma = pltpu.SemaphoreType.DMA
    return pl.pallas_call(
        functools.partial(kernel, n_ta, n_af, hours * nodes_dev * n_af),
        out_shape=(
            jax.ShapeDtypeStruct(features.shape, BF16),
            jax.ShapeDtypeStruct((width // n_af, width), F32),
        ),
        in_specs=[vmem, vmem, vmem, vmem, vmem, vmem, vmem, smem, smem, anywhere],
        out_specs=(anywhere, vmem),
        scratch_shapes=[
            pltpu.VMEM((hours_dev, 2, RIM, width), BF16),
            pltpu.VMEM((hours_dev, extended, width), BF16),
            pltpu.VMEM((hours_dev, PAIRS, BLOCK, 2 * nodes_dev), BF16),
            pltpu.VMEM((hours_dev, PAIRS, BLOCK + PADDED, extended), BF16),
            pltpu.VMEM((2, width, width), BF16),
            pltpu.VMEM((2, width, width), BF16),
            pltpu.VMEM((hours_dev, nodes_dev, width), BF16),
            pltpu.VMEM((hours, part, width), BF16),
            pltpu.VMEM((hours, part, width), BF16),
            pltpu.VMEM((hours * GROUP, hours * GROUP), F32),
            pltpu.VMEM((hours, part, width), BF16),
            pltpu.VMEM((width, width), F32),
            pltpu.VMEM((n_af, PADDED, width), BF16),
            pltpu.VMEM((n_af, PADDED, width), BF16),
            pltpu.VMEM((PADDED, width), F32),
            pltpu.VMEM((n_ta, PADDED, width), F32),
            dma((hours_dev, 2)),
            dma((hours_dev, 2)),
            dma((n_ta,)),
            dma((n_ta,)),
            dma((hours_dev, n_ta)),
            dma((hours_dev, n_ta)),
            dma((groups, n_ta)),
            dma((groups, n_ta)),
            dma((n_af,)),
            dma((n_af,)),
            dma((n_ta,)),
            dma((n_ta,)),
            dma((2,)),
        ],
        compiler_params=pltpu.CompilerParams(
            collective_id=0, has_side_effects=True, vmem_limit_bytes=48 * 2**20
        ),
    )(features, ws, wso, wt, wto, gain_s[None], gain_t[None], neighbours, degrees, cotangent)


def solution(mesh):
    return jax.shard_map(
        functools.partial(shards, mesh.shape["ta"], mesh.shape["af"]),
        mesh=mesh,
        in_specs=(
            P("ta", "af", None),
            P(),
            P(),
            P(),
            P(),
            P(),
            P(),
            P("af", None),
            P("af"),
            P("ta", "af", None),
        ),
        out_specs=(P("ta", "af", None), P("af", None)),
        check_vma=False,
    )
```

time: 335 us -> 78.5 us (0.23); the launches traced: 330 us -> 78.1 us
  blocking collectives: 118 us -> 0 us
  Pallas kernels: 0 us -> 68.1 us
  local copies, waits for them, and re-layouts: 68.5 us -> 9.38 us
  waiting for transfers between devices: 47.2 us -> 0 us
  starting transfers between devices: 36.5 us -> 0 us
  matrix products: 32.8 us -> 0 us
  other arithmetic: 25.2 us -> 0 us
    pallas_call x0 -> x1, Pallas kernels: none -> 68.1 us  [shards(): pl.pallas_call(functools.partial(kernel, n_ta, n_af, hours * nodes_dev *...]
    unnamed x1 -> x0, blocking collectives: 64.9 us -> none
    psum x1 -> x0, blocking collectives: 37.3 us -> none  [shards(): gradient = lax.psum(owned, 'ta')]
    dot_general x9 -> x0, matrix products: 32.8 us -> none  [the longest x1 9.9 us: shards(): jnp.einsum('hbnqk,hbknd->hbqnd', weights, selected[:, :, :, 1], preferred...]
    reshape x6 -> x0, local copies, waits for them, and re-layouts: 30 us -> none  [the longest x1 18.4 us: shards(): selected.reshape(hours_dev, blocks_dev, slots * block, 2, HEADS, head_dim)]
    all_to_all x1 -> x0, waiting for transfers between devices: 29.1 us -> none  [shards(): lax.all_to_all(projected_time, 'ta', split_axis=1, concat_axis=0, tiled=T...]
    unnamed x8 -> x0, starting transfers between devices: 23.6 us -> none
    gather x2 -> x0, local copies, waits for them, and re-layouts: 22.8 us -> none  [shards(): selected = stacked[:, local_index]]
  transfers between devices with their start and end apart: 11 -> 0, of which waited for: 3 -> 0; matrix products, arithmetic and copies ran while one was open for 1% -> 0% of each run, Pallas kernels for 0% -> 0%
where the time goes in v1:
time: 78.5 us; the launch traced here: 78.1 us
  Pallas kernels  68.1 us (87%)
  local copies, waits for them, and re-layouts  9.38 us (12%)
    pallas_call x1, Pallas kernels, shards(): pl.pallas_call(functools.partial(kernel, n_ta, n_af, hours * nodes_dev *...  68.1 us
    unnamed x20, local copies, waits for them, and re-layouts  8.69 us

profile of v1, /device:TPU:1, one launch (start us, length us, event | category | flops | bytes accessed | tf_op | source)
XLA Modules:
  0.0 78.1 jit_solution(11661150640824974611)
XLA Ops:
  0.6 0.0 copy-start.8
  0.6 0.7 broadcast_in_dim.6.gs_ref
  1.3 0.0 copy-done.8
  1.3 0.0 copy-start.6
  1.3 0.0 copy-start.7
  1.3 0.7 copy-done.6
  2.0 0.0 copy-done.7
  2.0 0.0 copy-start
  2.0 1.2 %copy-done = bf16[384,1152]{1,0:T(8,128)(2,1)S(1)} copy-done((bf16[384,1152]{1,0:T(8,128)(2,1)S(1)}, bf16[384,1152]{1,0:T(8,128)(2,1)}, u32[]{:S(2)}) %copy-start) | copy-done | bytes 884760
  3.2 0.0 copy-start.1
  3.2 1.2 %copy-done.1 = bf16[384,1152]{1,0:T(8,128)(2,1)S(1)} copy-done((bf16[384,1152]{1,0:T(8,128)(2,1)S(1)}, bf16[384,1152]{1,0:T(8,128)(2,1)}, u32[]{:S(2)}) %copy-start.1) | copy-done | bytes 884760
  4.4 0.0 copy-start.2
  4.4 1.1 %copy-done.2 = bf16[2,512,384]{2,1,0:T(8,128)(2,1)S(1)} copy-done((bf16[2,512,384]{2,1,0:T(8,128)(2,1)S(1)}, bf16[2,512,384]{2,1,0:T(8,128)(2,1)}, u32[]{:S(2)}) %copy-start.2) | copy-done | bytes 786456
  5.5 0.0 copy-start.3
  5.5 1.1 %copy-done.3 = bf16[2,512,384]{2,1,0:T(8,128)(2,1)S(1)} copy-done((bf16[2,512,384]{2,1,0:T(8,128)(2,1)S(1)}, bf16[2,512,384]{2,1,0:T(8,128)(2,1)}, u32[]{:S(2)}) %copy-start.3) | copy-done | bytes 786456
  6.6 0.0 copy-start.4
  6.6 1.0 %copy-done.4 = bf16[384,384]{1,0:T(8,128)(2,1)S(1)} copy-done((bf16[384,384]{1,0:T(8,128)(2,1)S(1)}, bf16[384,384]{1,0:T(8,128)(2,1)}, u32[]{:S(2)}) %copy-start.4) | copy-done | bytes 294936
  7.6 0.0 copy-start.5
  7.6 1.0 %copy-done.5 = bf16[384,384]{1,0:T(8,128)(2,1)S(1)} copy-done((bf16[384,384]{1,0:T(8,128)(2,1)S(1)}, bf16[384,384]{1,0:T(8,128)(2,1)}, u32[]{:S(2)}) %copy-start.5) | copy-done | bytes 294936
  8.5 68.1 %shard_map.113 = (bf16[2,512,384]{2,1,0:T(8,128)(2,1)S(1)}, f32[12,384]{1,0:T(8,128)S(1)}) custom-call(bf16[2,512,384]{2,1,0:T(8,128)(2,1)S(1)} %copy-done.2, bf16[384,1152]{1,0:T(8,128)(2,1)S(1)} %copy-done, bf16[384,384]{1,0:T(8,128)(2,1)S(1)} %copy-done.4, bf16[384,1152]{1,0:T(8,128)(2,1)S(1)} %copy-done.1, bf16[384,384]{1,0:T(8,128)(2,1)S(1)} %copy-done.5, ...), custom_call_target="tpu_custom_call" | custom-call | tf_op jit(solution)/shard_map/pallas_call | solution.py:335
  76.6 0.9 %copy.14 = bf16[2,512,384]{2,1,0:T(8,128)(2,1)} copy(bf16[2,512,384]{2,1,0:T(8,128)(2,1)S(1)} %get-tuple-element.4) | data formatting | bytes 1572864
  77.5 0.6 copy.15
  (1 shorter events, 0.0 us)
Async XLA Ops:
  0.6 0.7 copy-start.8
  1.3 0.7 copy-start.6
  1.3 0.7 copy-start.7
  2.0 1.2 %copy-start = (bf16[384,1152]{1,0:T(8,128)(2,1)S(1)}, bf16[384,1152]{1,0:T(8,128)(2,1)}, u32[]{:S(2)}) copy-start(bf16[384,1152]{1,0:T(8,128)(2,1)} %ws_ref.1) | copy-start | bytes 2654212
  3.2 1.2 %copy-start.1 = (bf16[384,1152]{1,0:T(8,128)(2,1)S(1)}, bf16[384,1152]{1,0:T(8,128)(2,1)}, u32[]{:S(2)}) copy-start(bf16[384,1152]{1,0:T(8,128)(2,1)} %wt_ref.1) | copy-start | bytes 2654212
  4.4 1.1 %copy-start.2 = (bf16[2,512,384]{2,1,0:T(8,128)(2,1)S(1)}, bf16[2,512,384]{2,1,0:T(8,128)(2,1)}, u32[]{:S(2)}) copy-start(bf16[2,512,384]{2,1,0:T(8,128)(2,1)} %x_ref.1) | copy-start | bytes 2359300
  5.5 1.1 %copy-start.3 = (bf16[2,512,384]{2,1,0:T(8,128)(2,1)S(1)}, bf16[2,512,384]{2,1,0:T(8,128)(2,1)}, u32[]{:S(2)}) copy-start(bf16[2,512,384]{2,1,0:T(8,128)(2,1)} %cot_ref.1) | copy-start | bytes 2359300
  6.6 1.0 %copy-start.4 = (bf16[384,384]{1,0:T(8,128)(2,1)S(1)}, bf16[384,384]{1,0:T(8,128)(2,1)}, u32[]{:S(2)}) copy-start(bf16[384,384]{1,0:T(8,128)(2,1)} %wso_ref.1) | copy-start | bytes 884740
  7.6 1.0 %copy-start.5 = (bf16[384,384]{1,0:T(8,128)(2,1)S(1)}, bf16[384,384]{1,0:T(8,128)(2,1)}, u32[]{:S(2)}) copy-start(bf16[384,384]{1,0:T(8,128)(2,1)} %wto_ref.1) | copy-start | bytes 884740

commit v2 on v1

--- a/solution.py
+++ b/solution.py
@@ -37,10 +37,34 @@
     return (rows * lax.rsqrt(mean_square + 1e-06) * gain).astype(BF16)
 
 
+def fold(tile):
+    widest = tile[:32]
+    for low in range(32, tile.shape[0], 32):
+        widest = jnp.maximum(widest, tile[low : low + 32])
+    widest = jnp.maximum(widest[:16], widest[16:])
+    return jnp.maximum(widest[:8], widest[8:])
+
+
+def powers_of_two(exponents):
+    return jnp.exp2(exponents.astype(BF16))
+
+
 def kernel(
     n_ta,
     n_af,
     tokens,
+    x_in,
+    ws_in,
+    wso_in,
+    wt_in,
+    wto_in,
+    gs_in,
+    gt_in,
+    nb_in,
+    dg_in,
+    cot_ref,
+    out_ref,
+    grad_ref,
     x_ref,
     ws_ref,
     wso_ref,
@@ -50,9 +74,6 @@
     gt_ref,
     nb_ref,
     dg_ref,
-    cot_ref,
-    out_ref,
-    grad_ref,
     halo,
     k_ext,
     q_diag,
@@ -63,8 +84,11 @@
     h_all,
     c_all,
     bias,
+    picks,
     out_staged,
     g_total,
+    pair_send,
+    pair_recv,
     g_send,
     g_recv,
     t_send,
@@ -77,15 +101,17 @@
     h_recv,
     o_send,
     o_recv,
+    pair_sem,
     gs_sem,
     gr_sem,
     ts_sem,
     tr_sem,
     own_sem,
+    in_sem,
 ):
     ta = lax.axis_index("ta")
     af = lax.axis_index("af")
-    hours_dev, nodes_dev, _ = x_ref.shape
+    hours_dev, nodes_dev, _ = x_in.shape
     part = nodes_dev // n_ta
     blocks_dev = nodes_dev // BLOCK
     hours = hours_dev * n_ta
@@ -104,10 +130,10 @@
         )
 
     def halo_right(h):
-        return to(ta, right, x_ref.at[h, pl.ds(nodes_dev - RIM, RIM)], halo.at[h, 0], halo_send.at[h, 0], halo_recv.at[h, 0])
+        return to(ta, right, x_in.at[h, pl.ds(nodes_dev - RIM, RIM)], halo.at[h, 0], halo_send.at[h, 0], halo_recv.at[h, 0])
 
     def halo_left(h):
-        return to(ta, left, x_ref.at[h, pl.ds(0, RIM)], halo.at[h, 1], halo_send.at[h, 1], halo_recv.at[h, 1])
+        return to(ta, left, x_in.at[h, pl.ds(0, RIM)], halo.at[h, 1], halo_send.at[h, 1], halo_recv.at[h, 1])
 
     def cot_copy(peer, slot):
         rows = pl.ds(pl.multiple_of(peer * part, part), part)
@@ -123,8 +149,26 @@
         src = out_staged.at[pl.ds(peer * hours_dev, hours_dev), rows]
         return to(peer, af, src, out_ref.at[:, there], o_send.at[g, peer], o_recv.at[g, slot])
 
-    def grad_copy(peer, slot):
-        return to(ta, peer, g_send.at[peer], g_recv.at[slot], gs_sem.at[peer], gr_sem.at[slot])
+    core = lax.rem(ta, 2)
+    partner = ta + 1 - 2 * core
+    owners = n_af // 2
+    holds = af // owners == core
+    pair_copy = to(partner, af, pair_send, pair_recv, pair_sem.at[0], pair_sem.at[1])
+
+    def grad_copy(k, owner, slot):
+        return to(ta, owner, g_send.at[k], g_recv.at[slot], gs_sem.at[k], gr_sem.at[slot])
+
+    def to_owners(act):
+        def step(i, carry):
+            k = lax.rem(af + i, owners)
+
+            @pl.when(core * owners + k != af)
+            def _():
+                act(k)
+
+            return carry
+
+        lax.fori_loop(0, owners, step, 0)
 
     def total_copy(peer, slot):
         return to(peer, af, t_send, t_recv.at[slot], ts_sem.at[peer], tr_sem.at[slot])
@@ -140,13 +184,33 @@
     others(n_ta, ta, lambda p: pl.semaphore_signal(barrier, inc=1, device_id=(p, af), device_id_type=MESH))
     others(n_af, af, lambda p: pl.semaphore_signal(barrier, inc=1, device_id=(ta, p), device_id_type=MESH))
 
+    loads = [
+        pltpu.make_async_copy(src, dst, in_sem.at[n])
+        for n, (src, dst) in enumerate(
+            [
+                (ws_in, ws_ref),
+                (x_in, x_ref),
+                (gs_in, gs_ref),
+                (nb_in, nb_ref),
+                (dg_in, dg_ref),
+                (wso_in, wso_ref),
+                (wt_in, wt_ref),
+                (wto_in, wto_ref),
+                (gt_in, gt_ref),
+            ]
+        )
+    ]
+    for load in loads:
+        load.start()
+    pl.semaphore_wait(barrier, n_ta + n_af - 2)
+    halo_right(0).start()
+    halo_left(0).start()
+    loads[0].wait()
     ws_t[0] = ws_ref[:, :WIDTH].T
     ws_t[1] = ws_ref[:, 2 * WIDTH :].T
     q_diag[...] = jnp.zeros_like(q_diag)
     v_ext[:, :, BLOCK:, :] = jnp.ones_like(v_ext[:, :, BLOCK:, :])
-
-    pl.semaphore_wait(barrier, n_ta + n_af - 2)
-    for h in range(hours_dev):
+    for h in range(1, hours_dev):
         halo_right(h).start()
         halo_left(h).start()
     others(n_ta, ta, lambda p: cot_copy(p, ta).start())
@@ -165,7 +229,7 @@
             v_ext[h, pair, :BLOCK, pl.ds(where, count)] = values[pair * BLOCK : (pair + 1) * BLOCK]
 
     def own_rows(h, carry):
-        rows = normed(x_ref[h].astype(F32), gs_ref[...])
+        rows = normed(x_ref[h].astype(F32), gs_ref[...][None])
         keys_values(h, rows, RIM)
         queries = (dot_nt(ws_t[0], rows) * SCORE_SCALE).astype(BF16)
         for pair in range(PAIRS):
@@ -177,15 +241,24 @@
                     ]
         return carry
 
+    for load in loads[1:5]:
+        load.wait()
     lax.fori_loop(0, hours_dev, own_rows, 0)
+    for load in loads[5:]:
+        load.wait()
 
     wt_t[0] = wt_ref[:, :WIDTH].T
     wt_t[1] = wt_ref[:, 2 * WIDTH :].T
     key_index = lax.broadcasted_iota(jnp.int32, bias.shape, 0)
-    query_index = lax.broadcasted_iota(jnp.int32, bias.shape, 1)
-    ahead = query_index // GROUP - key_index // GROUP
-    seen = (query_index % GROUP == key_index % GROUP) & (ahead >= 0) & (ahead < WIN)
+    query_index = lax.broadcasted_iota(jnp.int32, bias.shape, 1) % BLOCK
+    ahead = query_index // 8 - key_index // 8
+    seen = (query_index % 8 == key_index % 8) & (ahead >= 0) & (ahead < WIN)
     bias[...] = jnp.where(seen, 0.0, -EXCLUDED)
+    slot = lax.broadcasted_iota(jnp.int32, picks.shape, 0)
+    row = lax.broadcasted_iota(jnp.int32, picks.shape, 1)
+    inside = slot % PADDED
+    wanted = (inside < OWNED) & (slot // PADDED * OWNED + inside == row)
+    picks[...] = jnp.where(wanted, 1.0, 0.0).astype(BF16)
     g_total[...] = jnp.zeros_like(g_total)
 
     def spatial_block(h, i, carry):
@@ -208,12 +281,10 @@
             tiles = [scores[o * BLOCK : (o + 1) * BLOCK] for o in range(5)]
             largest = None
             for tile, extra in zip(tiles, penalty, strict=True):
-                here = jnp.max(tile, axis=0, keepdims=True) - extra
+                here = fold(tile) - extra
                 largest = here if largest is None else jnp.maximum(largest, here)
-            powers = [
-                jnp.exp2(tile - (largest + extra)).astype(BF16)
-                for tile, extra in zip(tiles, penalty, strict=True)
-            ]
+            largest = jnp.max(largest, axis=0, keepdims=True)
+            powers = [powers_of_two(tile - (largest + extra)) for tile, extra in zip(tiles, penalty, strict=True)]
             summed = dot(v_ext[h, pair, :, pl.ds(first, SPAN)], jnp.concatenate(powers, axis=0))
             inverse = 1.0 / summed[BLOCK : BLOCK + 1]
             half = BLOCK // 2
@@ -240,7 +311,7 @@
         halo_right(h).wait_recv()
         halo_left(h).wait_recv()
         for side in range(2):
-            rows = normed(halo[h, side].astype(F32), gs_ref[...])
+            rows = normed(halo[h, side].astype(F32), gs_ref[...][None])
             keys_values(h, rows, side * (RIM + nodes_dev))
         return lax.fori_loop(0, blocks_dev, functools.partial(spatial_block, h), carry)
 
@@ -251,34 +322,44 @@
     for h in range(hours_dev):
         others(n_ta, ta, lambda p, h=h: hidden_copy(p, h, p).wait_recv())
 
-    tokens_group = hours * GROUP
+    def split(slab):
+        return jnp.concatenate([slab[:, low : low + 8].reshape(BLOCK, WIDTH) for low in (0, 8)], axis=0)
+
+    def joined(rows):
+        return jnp.concatenate([rows[low : low + BLOCK].reshape(hours, 8, WIDTH) for low in (0, BLOCK)], axis=1)
 
     def temporal_group(g, carry):
         nodes = pl.ds(pl.multiple_of(g * GROUP, GROUP), GROUP)
-        hidden = h_all[:, nodes].reshape(tokens_group, WIDTH).astype(F32)
-        rows = normed(hidden, gt_ref[...])
+        hidden = split(h_all[:, nodes].astype(F32))
+        rows = normed(hidden, gt_ref[...][None])
         keys = dot(rows, wt_ref[:, WIDTH : 2 * WIDTH]).astype(BF16)
         queries = (dot_nt(wt_t[0], rows) * SCORE_SCALE).astype(BF16)
         values = dot_nt(wt_t[1], rows).astype(BF16)
         half = BLOCK // 2
-        blank = jnp.zeros((half, tokens_group), BF16)
-        ones = jnp.ones((PADDED, tokens_group), BF16)
+        blank = jnp.zeros((half, BLOCK), BF16)
+        ones = jnp.ones((PADDED, BLOCK), BF16)
         attended = []
-        for head in range(2 * PAIRS):
-            low = head * half
-            mine = queries[low : low + half]
-            padded = jnp.concatenate([mine, blank] if head % 2 == 0 else [blank, mine], axis=0)
-            pair = slice(head // 2 * BLOCK, (head // 2 + 1) * BLOCK)
-            scores = dot(keys[:, pair], padded) + bias[...]
-            largest = jnp.max(scores, axis=0, keepdims=True)
-            powers = jnp.exp2(scores - largest).astype(BF16)
-            summed = dot(jnp.concatenate([values[low : low + half], ones], axis=0), powers)
-            attended.append(summed[:half] * (1.0 / summed[half : half + 1]))
-        attended = jnp.concatenate(attended, axis=0)
-        cot = c_all[:, nodes].reshape(tokens_group, WIDTH)
-        g_total[...] += dot(attended.astype(BF16), cot)
-        mixed = dot(attended.T.astype(BF16), wto_ref[...])
-        out_staged[:, nodes] = (hidden + mixed).astype(BF16).reshape(hours, GROUP, WIDTH)
+        for eight in range(2):
+            these = slice(eight * BLOCK, (eight + 1) * BLOCK)
+            column = []
+            for pair in range(PAIRS):
+                heads = slice(pair * BLOCK, (pair + 1) * BLOCK)
+                mine = queries[heads, these]
+                diagonal = jnp.concatenate(
+                    [jnp.concatenate([mine[:half], blank], axis=1), jnp.concatenate([blank, mine[half:]], axis=1)], axis=0
+                )
+                scores = dot(keys[these, heads], diagonal) + bias[...]
+                largest = jnp.max(fold(scores), axis=0, keepdims=True)
+                powers = powers_of_two(scores - largest)
+                summed = dot(jnp.concatenate([values[heads, these], ones], axis=0), powers)
+                inverse = 1.0 / summed[BLOCK : BLOCK + 1]
+                column.append(summed[:half, :BLOCK] * inverse[:, :BLOCK])
+                column.append(summed[half:BLOCK, BLOCK:] * inverse[:, BLOCK:])
+            attended.append(jnp.concatenate(column, axis=0))
+        cot = split(c_all[:, nodes].astype(F32)).astype(BF16)
+        g_total[...] += dot(jnp.concatenate(attended, axis=1).astype(BF16), cot)
+        mixed = dot(jnp.concatenate([a.T for a in attended], axis=0).astype(BF16), wto_ref[...])
+        out_staged[:, nodes] = joined(hidden + mixed).astype(BF16)
         others(n_ta, ta, lambda p: out_copy(g, p, ta).start())
         return carry
 
@@ -291,19 +372,36 @@
     own_out.start()
 
     term = (g_total[...] * tokens ** (-0.5)).astype(BF16)
-    slot = lax.broadcasted_iota(jnp.int32, (n_af * PADDED, WIDTH), 0)
-    row = lax.broadcasted_iota(jnp.int32, (n_af * PADDED, WIDTH), 1)
-    inside = slot % PADDED
-    picks = (inside < OWNED) & (slot // PADDED * OWNED + inside == row)
-    picks = jnp.where(picks, 1.0, 0.0).astype(BF16)
-    g_send[...] = dot(picks, term).astype(BF16).reshape(n_af, PADDED, WIDTH)
-    others(n_af, af, lambda p: grad_copy(p, af).start())
-    g_recv[af] = g_send[af]
-    others(n_af, af, lambda p: grad_copy(p, p).wait_recv())
-    t_send[...] = jnp.sum(g_recv[...].astype(F32), axis=0)
-    others(n_ta, ta, lambda p: total_copy(p, ta).start())
-    t_recv[ta] = t_send[...]
-    others(n_ta, ta, lambda p: total_copy(p, p).wait_recv())
+
+    def terms_of(core):
+        rows = pl.ds(pl.multiple_of(core * owners * PADDED, PADDED), owners * PADDED)
+        return dot(picks[rows], term).reshape(owners, PADDED, WIDTH)
+
+    pair_send[...] = terms_of(1 - core).astype(BF16)
+    pair_copy.start()
+    mine = terms_of(core)
+    pair_copy.wait_recv()
+    g_send[...] = (mine + pair_recv[...].astype(F32)).astype(BF16)
+    to_owners(lambda k: grad_copy(k, core * owners + k, af).start())
+
+    @pl.when(holds)
+    def _():
+        g_recv[af] = g_send[lax.rem(af, owners)]
+        others(n_af, af, lambda p: grad_copy(0, p, p).wait_recv())
+        t_send[...] = jnp.sum(g_recv[...].astype(F32), axis=0)
+        others(n_ta, ta, lambda p: total_copy(p, ta // 2).start())
+        t_recv[ta // 2] = t_send[...]
+
+    def holder_wait(n, carry):
+        source = 2 * n + af // owners
+
+        @pl.when(source != ta)
+        def _():
+            total_copy(source, n).wait_recv()
+
+        return carry
+
+    lax.fori_loop(0, n_ta // 2, holder_wait, 0)
     grad_ref[...] = jnp.sum(t_recv[...], axis=0)[:OWNED]
 
     def out_waits(g, carry):
@@ -318,8 +416,12 @@
         halo_left(h).wait_send()
         others(n_ta, ta, lambda p, h=h: hidden_copy(p, h, ta).wait_send())
     others(n_ta, ta, lambda p: cot_copy(p, ta).wait_send())
-    others(n_af, af, lambda p: grad_copy(p, af).wait_send())
-    others(n_ta, ta, lambda p: total_copy(p, ta).wait_send())
+    pair_copy.wait_send()
+    to_owners(lambda k: grad_copy(k, core * owners + k, af).wait_send())
+
+    @pl.when(holds)
+    def _():
+        others(n_ta, ta, lambda p: total_copy(p, ta // 2).wait_send())
 
 
 def shards(n_ta, n_af, features, ws, wso, wt, wto, gain_s, gain_t, neighbours, degrees, cotangent):
@@ -329,7 +431,6 @@
     groups = part // GROUP
     extended = nodes_dev + 2 * RIM
     vmem = pl.BlockSpec(memory_space=pltpu.VMEM)
-    smem = pl.BlockSpec(memory_space=pltpu.SMEM)
     anywhere = pl.BlockSpec(memory_space=pl.ANY)
     dma = pltpu.SemaphoreType.DMA
     return pl.pallas_call(
@@ -338,9 +439,12 @@
             jax.ShapeDtypeStruct(features.shape, BF16),
             jax.ShapeDtypeStruct((width // n_af, width), F32),
         ),
-        in_specs=[vmem, vmem, vmem, vmem, vmem, vmem, vmem, smem, smem, anywhere],
+        in_specs=[anywhere] * 10,
         out_specs=(anywhere, vmem),
         scratch_shapes=[
+            *(pltpu.VMEM(a.shape, a.dtype) for a in (features, ws, wso, wt, wto, gain_s, gain_t)),
+            pltpu.SMEM(neighbours.shape, jnp.int32),
+            pltpu.SMEM(degrees.shape, jnp.int32),
             pltpu.VMEM((hours_dev, 2, RIM, width), BF16),
             pltpu.VMEM((hours_dev, extended, width), BF16),
             pltpu.VMEM((hours_dev, PAIRS, BLOCK, 2 * nodes_dev), BF16),
@@ -350,13 +454,16 @@
             pltpu.VMEM((hours_dev, nodes_dev, width), BF16),
             pltpu.VMEM((hours, part, width), BF16),
             pltpu.VMEM((hours, part, width), BF16),
-            pltpu.VMEM((hours * GROUP, hours * GROUP), F32),
+            pltpu.VMEM((BLOCK, 2 * BLOCK), F32),
+            pltpu.VMEM((n_af * PADDED, width), BF16),
             pltpu.VMEM((hours, part, width), BF16),
             pltpu.VMEM((width, width), F32),
-            pltpu.VMEM((n_af, PADDED, width), BF16),
+            pltpu.VMEM((n_af // 2, PADDED, width), BF16),
+            pltpu.VMEM((n_af // 2, PADDED, width), BF16),
+            pltpu.VMEM((n_af // 2, PADDED, width), BF16),
             pltpu.VMEM((n_af, PADDED, width), BF16),
             pltpu.VMEM((PADDED, width), F32),
-            pltpu.VMEM((n_ta, PADDED, width), F32),
+            pltpu.VMEM((n_ta // 2, PADDED, width), F32),
             dma((hours_dev, 2)),
             dma((hours_dev, 2)),
             dma((n_ta,)),
@@ -365,16 +472,18 @@
             dma((hours_dev, n_ta)),
             dma((groups, n_ta)),
             dma((groups, n_ta)),
-            dma((n_af,)),
+            dma((2,)),
+            dma((n_af // 2,)),
             dma((n_af,)),
             dma((n_ta,)),
-            dma((n_ta,)),
+            dma((n_ta // 2,)),
             dma((2,)),
+            dma((9,)),
         ],
         compiler_params=pltpu.CompilerParams(
-            collective_id=0, has_side_effects=True, vmem_limit_bytes=48 * 2**20
+            collective_id=0, has_side_effects=True, vmem_limit_bytes=63 * 2**20
         ),
-    )(features, ws, wso, wt, wto, gain_s[None], gain_t[None], neighbours, degrees, cotangent)
+    )(features, ws, wso, wt, wto, gain_s, gain_t, neighbours, degrees, cotangent)
 
 
 def solution(mesh):

time: 78.5 us -> 64.6 us (0.82)
  Pallas kernels: 68.1 us -> 61.1 us
  local copies, waits for them, and re-layouts: 9.38 us -> 2.71 us
    pallas_call x1, Pallas kernels: 68.1 us -> 61.1 us  [shards(): pl.pallas_call(functools.partial(kernel, n_ta, n_af, hours * nodes_dev *...]
    unnamed x20 -> x4, local copies, waits for them, and re-layouts: 8.69 us -> 2.71 us
where the time goes in v2:
time: 64.6 us; the launch traced here: 64.5 us
  Pallas kernels  61.1 us (95%)
  local copies, waits for them, and re-layouts  2.71 us (4%)
  between operations  0.65 us (1%)
    pallas_call x1, Pallas kernels, shards(): pl.pallas_call(functools.partial(kernel, n_ta, n_af, hours * nodes_dev *...  61.1 us
    unnamed x4, local copies, waits for them, and re-layouts  2.71 us

profile of v2, /device:TPU:1, one launch (start us, length us, event | category | flops | bytes accessed | tf_op | source)
XLA Modules:
  0.0 64.5 jit_solution(7931933749877305605)
XLA Ops:
  0.6 61.1 %shard_map.113 = (bf16[2,512,384]{2,1,0:T(8,128)(2,1)}, f32[12,384]{1,0:T(8,128)}) custom-call(bf16[2,512,384]{2,1,0:T(8,128)(2,1)} %x_in.1, bf16[384,1152]{1,0:T(8,128)(2,1)} %ws_in.1, bf16[384,384]{1,0:T(8,128)(2,1)} %wso_in.1, bf16[384,1152]{1,0:T(8,128)(2,1)} %wt_in.1, bf16[384,384]{1,0:T(8,128)(2,1)} %wto_in.1, f32[384]{0:T(512)} %gs_in.1, f32[384]{0:T(512)} %gt_in.1, ...), custom_call_target="tpu_custom_call" | custom-call | tf_op jit(solution)/shard_map/pallas_call | solution.py:436
  61.8 0.0 copy-start
  61.8 2.1 %copy.14 = bf16[2,512,384]{2,1,0:T(8,128)(2,1)} copy(bf16[2,512,384]{2,1,0:T(8,128)(2,1)} %get-tuple-element.4) | data formatting | bytes 1572864
  63.9 0.0 copy-done
  63.9 0.6 copy.15
Async XLA Ops:
  61.8 2.1 %copy-start = (f32[12,384]{1,0:T(8,128)S(1)}, f32[12,384]{1,0:T(8,128)}, u32[]{:S(2)}) copy-start(f32[12,384]{1,0:T(8,128)} %get-tuple-element.5) | copy-start | bytes 55300

commit v3 on v2

--- a/solution.py
+++ b/solution.py
@@ -12,11 +12,14 @@
 BF16 = jnp.bfloat16
 
 WIDTH = 384
+HEADS = 6
+HEAD = 64
 PAIRS = 3
 BLOCK = 128
 RIM = 256
 SPAN = 640
 WIN = 12
+TURNS = (2, 1, 3, 0)
 GROUP = 16
 OWNED = 12
 PADDED = 16
@@ -47,6 +50,22 @@
 
 def powers_of_two(exponents):
     return jnp.exp2(exponents.astype(BF16))
+
+
+def staggered(units):
+    count = len(units)
+    for step in range(count + 2):
+        if step < count:
+            (scores, _, _, _), pair = units[step]
+            scores(pair)
+        if 0 <= step - 1 < count:
+            (_, powers, _, _), pair = units[step - 1]
+            powers(pair)
+        if 0 <= step - 2:
+            (_, _, sums, end), pair = units[step - 2]
+            sums(pair)
+            if pair == PAIRS - 1:
+                end()
 
 
 def kernel(
@@ -209,7 +228,7 @@
     ws_t[0] = ws_ref[:, :WIDTH].T
     ws_t[1] = ws_ref[:, 2 * WIDTH :].T
     q_diag[...] = jnp.zeros_like(q_diag)
-    v_ext[:, :, BLOCK:, :] = jnp.ones_like(v_ext[:, :, BLOCK:, :])
+    v_ext[:, :, HEAD:, :] = jnp.ones_like(v_ext[:, :, HEAD:, :])
     for h in range(1, hours_dev):
         halo_right(h).start()
         halo_left(h).start()
@@ -225,8 +244,8 @@
         count = rows_normed.shape[0]
         k_ext[h, pl.ds(where, count), :] = dot(rows_normed, ws_ref[:, WIDTH : 2 * WIDTH]).astype(BF16)
         values = dot_nt(ws_t[1], rows_normed).astype(BF16)
-        for pair in range(PAIRS):
-            v_ext[h, pair, :BLOCK, pl.ds(where, count)] = values[pair * BLOCK : (pair + 1) * BLOCK]
+        for head in range(HEADS):
+            v_ext[h, head, :HEAD, pl.ds(where, count)] = values[head * HEAD : (head + 1) * HEAD]
 
     def own_rows(h, carry):
         rows = normed(x_ref[h].astype(F32), gs_ref[...][None])
@@ -261,9 +280,8 @@
     picks[...] = jnp.where(wanted, 1.0, 0.0).astype(BF16)
     g_total[...] = jnp.zeros_like(g_total)
 
-    def spatial_block(h, i, carry):
-        turn = jnp.where(i == 0, 2, jnp.where(i == 1, 1, jnp.where(i == 2, 3, 0)))
-        b = lax.rem(ta // 2 + turn, blocks_dev)
+    def spatial_turn(h, turn):
+        b = lax.rem(ta // 2 + TURNS[turn], blocks_dev)
         first = pl.multiple_of(b * BLOCK, BLOCK)
         penalty = []
         for o in range(5):
@@ -272,40 +290,45 @@
                 hit = (nb_ref[b, j] == af * blocks_dev + b + (o - 2)) & (j < dg_ref[b])
                 listed = listed | hit.astype(jnp.int32)
             penalty.append((1 - listed).astype(F32) * EXCLUDED)
+        cuts = (((0, 128, 0), (128, 256, 1), (256, 320, 2)), ((0, 64, 2), (64, 192, 3), (192, 320, 4)))
+        held = {}
         attended = []
-        for pair in range(PAIRS):
+
+        def scores(pair):
             columns = slice(pair * BLOCK, (pair + 1) * BLOCK)
-            keys = k_ext[h, pl.ds(first, SPAN), columns]
             queries = q_diag[h, pair, :, pl.ds(pl.multiple_of(b * 2 * BLOCK, 2 * BLOCK), 2 * BLOCK)]
-            scores = dot(keys, queries)
-            tiles = [scores[o * BLOCK : (o + 1) * BLOCK] for o in range(5)]
-            largest = None
-            for tile, extra in zip(tiles, penalty, strict=True):
-                here = fold(tile) - extra
-                largest = here if largest is None else jnp.maximum(largest, here)
-            largest = jnp.max(largest, axis=0, keepdims=True)
-            powers = [powers_of_two(tile - (largest + extra)) for tile, extra in zip(tiles, penalty, strict=True)]
-            summed = dot(v_ext[h, pair, :, pl.ds(first, SPAN)], jnp.concatenate(powers, axis=0))
-            inverse = 1.0 / summed[BLOCK : BLOCK + 1]
-            half = BLOCK // 2
-            attended.append(summed[:half, :BLOCK] * inverse[:, :BLOCK])
-            attended.append(summed[half:BLOCK, BLOCK:] * inverse[:, BLOCK:])
-        attended = jnp.concatenate(attended, axis=0).T.astype(BF16)
-        mixed = dot(attended, wso_ref[...])
-        hidden = (x_ref[h, pl.ds(first, BLOCK)].astype(F32) + mixed).astype(BF16)
-        staged[h, pl.ds(first, BLOCK)] = hidden
-        for k in range(BLOCK // part):
-            peer = b * (BLOCK // part) + k
-
-            @pl.when(peer != ta)
-            def _():
-                hidden_copy(peer, h, ta).start()
-
-            @pl.when(peer == ta)
-            def _():
-                h_all[ta * hours_dev + h] = hidden[k * part : (k + 1) * part]
-
-        return carry
+            tiles = []
+            for part_of, cut in enumerate(cuts):
+                start = pl.multiple_of(first + part_of * (SPAN // 2), HEAD)
+                product = dot(k_ext[h, pl.ds(start, SPAN // 2), columns], queries)
+                tiles += [(product[low:high], penalty[o]) for low, high, o in cut]
+            largest = functools.reduce(jnp.maximum, [fold(tile) - extra for tile, extra in tiles])
+            held[pair] = tiles, jnp.max(largest, axis=0, keepdims=True)
+
+        def powers(pair):
+            tiles, largest = held[pair]
+            held[pair] = jnp.concatenate([powers_of_two(tile - (largest + extra)) for tile, extra in tiles], axis=0)
+
+        def sums(pair):
+            weights = held.pop(pair)
+            for k in range(2):
+                summed = dot(v_ext[h, 2 * pair + k, :, pl.ds(first, SPAN)], weights[:, k * BLOCK : (k + 1) * BLOCK])
+                attended.append(summed[:HEAD] * (1.0 / summed[HEAD : HEAD + 1]))
+
+        def end():
+            rows = jnp.concatenate(attended, axis=0).T.astype(BF16)
+            mixed = dot(rows, wso_ref[...])
+            hidden = (x_ref[h, pl.ds(first, BLOCK)].astype(F32) + mixed).astype(BF16)
+            staged[h, pl.ds(first, BLOCK)] = hidden
+            if TURNS[turn]:
+                for k in range(2):
+                    hidden_copy(2 * b + k, h, ta).start()
+            else:
+                hidden_copy(partner, h, ta).start()
+                mine = pl.ds(pl.multiple_of(ta * part, part), part)
+                h_all[ta * hours_dev + h] = staged[h, mine]
+
+        return scores, powers, sums, end
 
     def spatial_hour(h, carry):
         halo_right(h).wait_recv()
@@ -313,7 +336,10 @@
         for side in range(2):
             rows = normed(halo[h, side].astype(F32), gs_ref[...][None])
             keys_values(h, rows, side * (RIM + nodes_dev))
-        return lax.fori_loop(0, blocks_dev, functools.partial(spatial_block, h), carry)
+        turns = [spatial_turn(h, turn) for turn in range(blocks_dev)]
+        units = [(turn, pair) for turn in turns for pair in range(PAIRS)]
+        staggered(units)
+        return carry
 
     lax.fori_loop(0, hours_dev, spatial_hour, 0)
 
@@ -335,32 +361,51 @@
         keys = dot(rows, wt_ref[:, WIDTH : 2 * WIDTH]).astype(BF16)
         queries = (dot_nt(wt_t[0], rows) * SCORE_SCALE).astype(BF16)
         values = dot_nt(wt_t[1], rows).astype(BF16)
-        half = BLOCK // 2
-        blank = jnp.zeros((half, BLOCK), BF16)
+        blank = jnp.zeros((HEAD, BLOCK), BF16)
         ones = jnp.ones((PADDED, BLOCK), BF16)
         attended = []
-        for eight in range(2):
+
+        def eight_nodes(eight):
             these = slice(eight * BLOCK, (eight + 1) * BLOCK)
+            held = {}
             column = []
-            for pair in range(PAIRS):
+
+            def scores(pair):
                 heads = slice(pair * BLOCK, (pair + 1) * BLOCK)
                 mine = queries[heads, these]
                 diagonal = jnp.concatenate(
-                    [jnp.concatenate([mine[:half], blank], axis=1), jnp.concatenate([blank, mine[half:]], axis=1)], axis=0
+                    [jnp.concatenate([mine[:HEAD], blank], axis=1), jnp.concatenate([blank, mine[HEAD:]], axis=1)], axis=0
                 )
-                scores = dot(keys[these, heads], diagonal) + bias[...]
-                largest = jnp.max(fold(scores), axis=0, keepdims=True)
-                powers = powers_of_two(scores - largest)
-                summed = dot(jnp.concatenate([values[heads, these], ones], axis=0), powers)
-                inverse = 1.0 / summed[BLOCK : BLOCK + 1]
-                column.append(summed[:half, :BLOCK] * inverse[:, :BLOCK])
-                column.append(summed[half:BLOCK, BLOCK:] * inverse[:, BLOCK:])
-            attended.append(jnp.concatenate(column, axis=0))
+                product = dot(keys[these, heads], diagonal) + bias[...]
+                held[pair] = product, jnp.max(fold(product), axis=0, keepdims=True)
+
+            def powers(pair):
+                product, largest = held[pair]
+                held[pair] = powers_of_two(product - largest)
+
+            def sums(pair):
+                weights = held.pop(pair)
+                for k in range(2):
+                    low = (2 * pair + k) * HEAD
+                    summed = dot(
+                        jnp.concatenate([values[low : low + HEAD, these], ones], axis=0),
+                        weights[:, k * BLOCK : (k + 1) * BLOCK],
+                    )
+                    column.append(summed[:HEAD] * (1.0 / summed[HEAD : HEAD + 1]))
+
+            def end():
+                attended.append(jnp.concatenate(column, axis=0))
+
+            return scores, powers, sums, end
+
+        sets = [eight_nodes(eight) for eight in range(2)]
+        staggered([(nodes_set, pair) for nodes_set in sets for pair in range(PAIRS)])
         cot = split(c_all[:, nodes].astype(F32)).astype(BF16)
         g_total[...] += dot(jnp.concatenate(attended, axis=1).astype(BF16), cot)
         mixed = dot(jnp.concatenate([a.T for a in attended], axis=0).astype(BF16), wto_ref[...])
         out_staged[:, nodes] = joined(hidden + mixed).astype(BF16)
-        others(n_ta, ta, lambda p: out_copy(g, p, ta).start())
+        for i in range(1, n_ta):
+            out_copy(g, lax.rem(ta + i, n_ta), ta).start()
         return carry
 
     lax.fori_loop(0, groups, temporal_group, 0)
@@ -402,7 +447,7 @@
         return carry
 
     lax.fori_loop(0, n_ta // 2, holder_wait, 0)
-    grad_ref[...] = jnp.sum(t_recv[...], axis=0)[:OWNED]
+    grad_ref[...] = t_recv[...]
 
     def out_waits(g, carry):
         others(n_ta, ta, lambda p: out_copy(g, p, p).wait_recv())
@@ -424,6 +469,23 @@
         others(n_ta, ta, lambda p: total_copy(p, ta // 2).wait_send())
 
 
+def closing(pieces, made_ref, terms_ref, out_ref, grad_ref, sems):
+    hours_dev, nodes_dev, _ = made_ref.shape
+    size = nodes_dev // pieces
+    copies = [
+        pltpu.make_async_copy(
+            made_ref.at[h, pl.ds(n * size, size)], out_ref.at[h, pl.ds(n * size, size)], sems.at[h, n]
+        )
+        for h in range(hours_dev)
+        for n in range(pieces)
+    ]
+    for copy in copies:
+        copy.start()
+    grad_ref[...] = jnp.sum(terms_ref[...], axis=0)[:OWNED]
+    for copy in copies:
+        copy.wait()
+
+
 def shards(n_ta, n_af, features, ws, wso, wt, wto, gain_s, gain_t, neighbours, degrees, cotangent):
     hours_dev, nodes_dev, width = features.shape
     part = nodes_dev // n_ta
@@ -433,11 +495,11 @@
     vmem = pl.BlockSpec(memory_space=pltpu.VMEM)
     anywhere = pl.BlockSpec(memory_space=pl.ANY)
     dma = pltpu.SemaphoreType.DMA
-    return pl.pallas_call(
+    output, terms = pl.pallas_call(
         functools.partial(kernel, n_ta, n_af, hours * nodes_dev * n_af),
         out_shape=(
             jax.ShapeDtypeStruct(features.shape, BF16),
-            jax.ShapeDtypeStruct((width // n_af, width), F32),
+            jax.ShapeDtypeStruct((n_ta // 2, PADDED, width), F32),
         ),
         in_specs=[anywhere] * 10,
         out_specs=(anywhere, vmem),
@@ -448,7 +510,7 @@
             pltpu.VMEM((hours_dev, 2, RIM, width), BF16),
             pltpu.VMEM((hours_dev, extended, width), BF16),
             pltpu.VMEM((hours_dev, PAIRS, BLOCK, 2 * nodes_dev), BF16),
-            pltpu.VMEM((hours_dev, PAIRS, BLOCK + PADDED, extended), BF16),
+            pltpu.VMEM((hours_dev, HEADS, HEAD + PADDED, extended), BF16),
             pltpu.VMEM((2, width, width), BF16),
             pltpu.VMEM((2, width, width), BF16),
             pltpu.VMEM((hours_dev, nodes_dev, width), BF16),
@@ -484,6 +546,18 @@
             collective_id=0, has_side_effects=True, vmem_limit_bytes=63 * 2**20
         ),
     )(features, ws, wso, wt, wto, gain_s, gain_t, neighbours, degrees, cotangent)
+    pieces = 8
+    return pl.pallas_call(
+        functools.partial(closing, pieces),
+        out_shape=(
+            jax.ShapeDtypeStruct(features.shape, BF16),
+            jax.ShapeDtypeStruct((width // n_af, width), F32),
+        ),
+        in_specs=[anywhere, vmem],
+        out_specs=(anywhere, vmem),
+        scratch_shapes=[dma((hours_dev, pieces))],
+        compiler_params=pltpu.CompilerParams(vmem_limit_bytes=63 * 2**20),
+    )(output, terms)
 
 
 def solution(mesh):

time: 64.6 us -> 82.4 us (1.28)
  Pallas kernels: 61.1 us -> 81.7 us
  local copies, waits for them, and re-layouts: 2.71 us -> 0 us
    pallas_call x0 -> x1, Pallas kernels: none -> 26.6 us  [shards(): pl.pallas_call(functools.partial(closing, pieces), out_shape=(jax.ShapeDt...]
    pallas_call x1, Pallas kernels: 61.1 us -> 55.1 us  [shards(): pl.pallas_call(functools.partial(kernel, n_ta, n_af, hours * nodes_dev *...]
    unnamed x4 -> x0, local copies, waits for them, and re-layouts: 2.71 us -> none
where the time goes in v3:
time: 82.4 us; the launch traced here: 82.3 us
  Pallas kernels  81.7 us (99%)
    pallas_call x1, Pallas kernels, shards(): pl.pallas_call(functools.partial(kernel, n_ta, n_af, hours * nodes_dev *...  55.1 us
    pallas_call x1, Pallas kernels, shards(): pl.pallas_call(functools.partial(closing, pieces), out_shape=(jax.ShapeDt...  26.6 us

profile of v3, /device:TPU:1, one launch (start us, length us, event | category | flops | bytes accessed | tf_op | source)
XLA Modules:
  0.0 82.3 jit_solution(3277897768174907316)
XLA Ops:
  0.6 55.1 %shard_map.113 = (bf16[2,512,384]{2,1,0:T(8,128)(2,1)}, f32[4,16,384]{2,1,0:T(8,128)}) custom-call(bf16[2,512,384]{2,1,0:T(8,128)(2,1)} %x_in.1, bf16[384,1152]{1,0:T(8,128)(2,1)} %ws_in.1, bf16[384,384]{1,0:T(8,128)(2,1)} %wso_in.1, bf16[384,1152]{1,0:T(8,128)(2,1)} %wt_in.1, bf16[384,384]{1,0:T(8,128)(2,1)} %wto_in.1, f32[384]{0:T(512)} %gs_in.1, ...), custom_call_target="tpu_custom_call" | custom-call | tf_op jit(solution)/shard_map/pallas_call | solution.py:498
  55.7 26.6 %shard_map.114 = (bf16[2,512,384]{2,1,0:T(8,128)(2,1)}, f32[12,384]{1,0:T(8,128)}) custom-call(bf16[2,512,384]{2,1,0:T(8,128)(2,1)} %get-tuple-element.4.made_ref, f32[4,16,384]{2,1,0:T(8,128)} %get-tuple-element.5.terms_ref), custom_call_target="tpu_custom_call" | custom-call | tf_op jit(solution)/shard_map/pallas_call | solution.py:550

commit v4 on v3

--- a/solution.py
+++ b/solution.py
@@ -447,7 +447,7 @@
         return carry
 
     lax.fori_loop(0, n_ta // 2, holder_wait, 0)
-    grad_ref[...] = t_recv[...]
+    grad_ref[...] = jnp.sum(t_recv[...], axis=0)[:OWNED]
 
     def out_waits(g, carry):
         others(n_ta, ta, lambda p: out_copy(g, p, p).wait_recv())
@@ -469,23 +469,6 @@
         others(n_ta, ta, lambda p: total_copy(p, ta // 2).wait_send())
 
 
-def closing(pieces, made_ref, terms_ref, out_ref, grad_ref, sems):
-    hours_dev, nodes_dev, _ = made_ref.shape
-    size = nodes_dev // pieces
-    copies = [
-        pltpu.make_async_copy(
-            made_ref.at[h, pl.ds(n * size, size)], out_ref.at[h, pl.ds(n * size, size)], sems.at[h, n]
-        )
-        for h in range(hours_dev)
-        for n in range(pieces)
-    ]
-    for copy in copies:
-        copy.start()
-    grad_ref[...] = jnp.sum(terms_ref[...], axis=0)[:OWNED]
-    for copy in copies:
-        copy.wait()
-
-
 def shards(n_ta, n_af, features, ws, wso, wt, wto, gain_s, gain_t, neighbours, degrees, cotangent):
     hours_dev, nodes_dev, width = features.shape
     part = nodes_dev // n_ta
@@ -495,11 +478,11 @@
     vmem = pl.BlockSpec(memory_space=pltpu.VMEM)
     anywhere = pl.BlockSpec(memory_space=pl.ANY)
     dma = pltpu.SemaphoreType.DMA
-    output, terms = pl.pallas_call(
+    return pl.pallas_call(
         functools.partial(kernel, n_ta, n_af, hours * nodes_dev * n_af),
         out_shape=(
             jax.ShapeDtypeStruct(features.shape, BF16),
-            jax.ShapeDtypeStruct((n_ta // 2, PADDED, width), F32),
+            jax.ShapeDtypeStruct((width // n_af, width), F32),
         ),
         in_specs=[anywhere] * 10,
         out_specs=(anywhere, vmem),
@@ -546,18 +529,6 @@
             collective_id=0, has_side_effects=True, vmem_limit_bytes=63 * 2**20
         ),
     )(features, ws, wso, wt, wto, gain_s, gain_t, neighbours, degrees, cotangent)
-    pieces = 8
-    return pl.pallas_call(
-        functools.partial(closing, pieces),
-        out_shape=(
-            jax.ShapeDtypeStruct(features.shape, BF16),
-            jax.ShapeDtypeStruct((width // n_af, width), F32),
-        ),
-        in_specs=[anywhere, vmem],
-        out_specs=(anywhere, vmem),
-        scratch_shapes=[dma((hours_dev, pieces))],
-        compiler_params=pltpu.CompilerParams(vmem_limit_bytes=63 * 2**20),
-    )(output, terms)
 
 
 def solution(mesh):

time: 82.4 us -> 58.9 us (0.71)
  Pallas kernels: 81.7 us -> 55.5 us
  local copies, waits for them, and re-layouts: 0 us -> 2.71 us
    pallas_call x1 -> x0, Pallas kernels: 26.6 us -> none  [shards(): pl.pallas_call(functools.partial(closing, pieces), out_shape=(jax.ShapeDt...]
    unnamed x0 -> x4, local copies, waits for them, and re-layouts: none -> 2.71 us
where the time goes in v4:
time: 58.9 us; the launch traced here: 58.8 us
  Pallas kernels  55.5 us (94%)
  local copies, waits for them, and re-layouts  2.71 us (5%)
  between operations  0.65 us (1%)
    pallas_call x1, Pallas kernels, shards(): pl.pallas_call(functools.partial(kernel, n_ta, n_af, hours * nodes_dev *...  55.5 us
    unnamed x4, local copies, waits for them, and re-layouts  2.71 us

profile of v4, /device:TPU:1, one launch (start us, length us, event | category | flops | bytes accessed | tf_op | source)
XLA Modules:
  0.0 58.8 jit_solution(2226660391544956384)
XLA Ops:
  0.6 55.5 %shard_map.113 = (bf16[2,512,384]{2,1,0:T(8,128)(2,1)}, f32[12,384]{1,0:T(8,128)}) custom-call(bf16[2,512,384]{2,1,0:T(8,128)(2,1)} %x_in.1, bf16[384,1152]{1,0:T(8,128)(2,1)} %ws_in.1, bf16[384,384]{1,0:T(8,128)(2,1)} %wso_in.1, bf16[384,1152]{1,0:T(8,128)(2,1)} %wt_in.1, bf16[384,384]{1,0:T(8,128)(2,1)} %wto_in.1, f32[384]{0:T(512)} %gs_in.1, f32[384]{0:T(512)} %gt_in.1, ...), custom_call_target="tpu_custom_call" | custom-call | tf_op jit(solution)/shard_map/pallas_call | solution.py:481
  56.1 0.0 copy-start
  56.1 2.1 %copy.14 = bf16[2,512,384]{2,1,0:T(8,128)(2,1)} copy(bf16[2,512,384]{2,1,0:T(8,128)(2,1)} %get-tuple-element.4) | data formatting | bytes 1572864
  58.2 0.0 copy-done
  58.2 0.6 %copy.15 = f32[12,384]{1,0:T(8,128)} copy(f32[12,384]{1,0:T(8,128)S(1)} %copy-done) | data formatting | bytes 36864
Async XLA Ops:
  56.1 2.1 %copy-start = (f32[12,384]{1,0:T(8,128)S(1)}, f32[12,384]{1,0:T(8,128)}, u32[]{:S(2)}) copy-start(f32[12,384]{1,0:T(8,128)} %get-tuple-element.5) | copy-start | bytes 55300

commit v5 on v4

--- a/solution.py
+++ b/solution.py
@@ -19,7 +19,6 @@
 RIM = 256
 SPAN = 640
 WIN = 12
-TURNS = (2, 1, 3, 0)
 GROUP = 16
 OWNED = 12
 PADDED = 16
@@ -102,6 +101,7 @@
     staged,
     h_all,
     c_all,
+    att,
     bias,
     picks,
     out_staged,
@@ -135,6 +135,8 @@
     blocks_dev = nodes_dev // BLOCK
     hours = hours_dev * n_ta
     groups = part // GROUP
+    core = lax.rem(ta, 2)
+    partner = ta + 1 - 2 * core
     right = lax.rem(af + 1, n_af)
     left = lax.rem(af + n_af - 1, n_af)
 
@@ -154,28 +156,46 @@
     def halo_left(h):
         return to(ta, left, x_in.at[h, pl.ds(0, RIM)], halo.at[h, 1], halo_send.at[h, 1], halo_recv.at[h, 1])
 
-    def cot_copy(peer, slot):
-        rows = pl.ds(pl.multiple_of(peer * part, part), part)
-        return to(peer, af, cot_ref.at[:, rows], c_all.at[pl.ds(slot * hours_dev, hours_dev)], c_send.at[peer], c_recv.at[slot])
-
-    def hidden_copy(peer, h, slot):
-        rows = pl.ds(pl.multiple_of(peer * part, part), part)
-        return to(peer, af, staged.at[h, rows], h_all.at[slot * hours_dev + h], h_send.at[h, peer], h_recv.at[h, slot])
+    def slices(b, peer):
+        return pl.ds(pl.multiple_of(b * BLOCK + peer * GROUP, GROUP), GROUP)
+
+    def gathered(b):
+        return pl.ds(pl.multiple_of(b * GROUP, GROUP), GROUP)
+
+    def cot_copy(b, peer, slot):
+        there = c_all.at[pl.ds(slot * hours_dev, hours_dev), gathered(b)]
+        return to(peer, af, cot_ref.at[:, slices(b, peer)], there, c_send.at[b], c_recv.at[b])
+
+    def hidden_copy(b, peer, h, slot):
+        there = h_all.at[slot * hours_dev + h, gathered(b)]
+        return to(peer, af, staged.at[h, slices(b, peer)], there, h_send.at[b], h_recv.at[b])
 
     def out_copy(g, peer, slot):
-        rows = pl.ds(pl.multiple_of(g * GROUP, GROUP), GROUP)
-        there = pl.ds(pl.multiple_of(slot * part + g * GROUP, GROUP), GROUP)
-        src = out_staged.at[pl.ds(peer * hours_dev, hours_dev), rows]
-        return to(peer, af, src, out_ref.at[:, there], o_send.at[g, peer], o_recv.at[g, slot])
-
-    core = lax.rem(ta, 2)
-    partner = ta + 1 - 2 * core
+        src = out_staged.at[pl.ds(peer * hours_dev, hours_dev), gathered(g)]
+        return to(peer, af, src, out_ref.at[:, slices(g, slot)], o_send.at[g], o_recv.at[g])
+
+    slabs = (pl.ds(0, (n_ta - 1) * hours_dev), pl.ds(0, GROUP))
+
+    def slabs_in(sem):
+        to(partner, af, c_all.at[slabs], h_all.at[slabs], own_sem.at[0, 0], sem).wait_recv()
+
+    def slabs_out(sem):
+        to(partner, af, c_all.at[slabs], h_all.at[slabs], sem, own_sem.at[0, 0]).wait_send()
+
+    def own_cot(b):
+        there = c_all.at[pl.ds(ta * hours_dev, hours_dev), gathered(b)]
+        return pltpu.make_async_copy(cot_ref.at[:, slices(b, ta)], there, own_sem.at[0, b])
+
+    def own_out(g):
+        src = out_staged.at[pl.ds(ta * hours_dev, hours_dev), gathered(g)]
+        return pltpu.make_async_copy(src, out_ref.at[:, slices(g, ta)], own_sem.at[1, g])
+
     owners = n_af // 2
     holds = af // owners == core
     pair_copy = to(partner, af, pair_send, pair_recv, pair_sem.at[0], pair_sem.at[1])
 
     def grad_copy(k, owner, slot):
-        return to(ta, owner, g_send.at[k], g_recv.at[slot], gs_sem.at[k], gr_sem.at[slot])
+        return to(ta, owner, g_send.at[k], g_recv.at[slot], gs_sem.at[0], gr_sem.at[0])
 
     def to_owners(act):
         def step(i, carry):
@@ -190,7 +210,7 @@
         lax.fori_loop(0, owners, step, 0)
 
     def total_copy(peer, slot):
-        return to(peer, af, t_send, t_recv.at[slot], ts_sem.at[peer], tr_sem.at[slot])
+        return to(peer, af, t_send, t_recv.at[slot], ts_sem.at[0], tr_sem.at[0])
 
     def others(count, me, act):
         def step(i, carry):
@@ -232,13 +252,9 @@
     for h in range(1, hours_dev):
         halo_right(h).start()
         halo_left(h).start()
-    others(n_ta, ta, lambda p: cot_copy(p, ta).start())
-    own_cot = pltpu.make_async_copy(
-        cot_ref.at[:, pl.ds(pl.multiple_of(ta * part, part), part)],
-        c_all.at[pl.ds(ta * hours_dev, hours_dev)],
-        own_sem.at[0],
-    )
-    own_cot.start()
+    for b in range(blocks_dev):
+        others(n_ta, ta, lambda p, b=b: cot_copy(b, p, ta).start())
+        own_cot(b).start()
 
     def keys_values(h, rows_normed, where):
         count = rows_normed.shape[0]
@@ -281,8 +297,8 @@
     g_total[...] = jnp.zeros_like(g_total)
 
     def spatial_turn(h, turn):
-        b = lax.rem(ta // 2 + TURNS[turn], blocks_dev)
-        first = pl.multiple_of(b * BLOCK, BLOCK)
+        b = turn
+        first = b * BLOCK
         penalty = []
         for o in range(5):
             listed = jnp.int32(0)
@@ -296,10 +312,10 @@
 
         def scores(pair):
             columns = slice(pair * BLOCK, (pair + 1) * BLOCK)
-            queries = q_diag[h, pair, :, pl.ds(pl.multiple_of(b * 2 * BLOCK, 2 * BLOCK), 2 * BLOCK)]
+            queries = q_diag[h, pair, :, pl.ds(b * 2 * BLOCK, 2 * BLOCK)]
             tiles = []
             for part_of, cut in enumerate(cuts):
-                start = pl.multiple_of(first + part_of * (SPAN // 2), HEAD)
+                start = first + part_of * (SPAN // 2)
                 product = dot(k_ext[h, pl.ds(start, SPAN // 2), columns], queries)
                 tiles += [(product[low:high], penalty[o]) for low, high, o in cut]
             largest = functools.reduce(jnp.maximum, [fold(tile) - extra for tile, extra in tiles])
@@ -320,13 +336,9 @@
             mixed = dot(rows, wso_ref[...])
             hidden = (x_ref[h, pl.ds(first, BLOCK)].astype(F32) + mixed).astype(BF16)
             staged[h, pl.ds(first, BLOCK)] = hidden
-            if TURNS[turn]:
-                for k in range(2):
-                    hidden_copy(2 * b + k, h, ta).start()
-            else:
-                hidden_copy(partner, h, ta).start()
-                mine = pl.ds(pl.multiple_of(ta * part, part), part)
-                h_all[ta * hours_dev + h] = staged[h, mine]
+            for i in range(1, n_ta):
+                hidden_copy(b, lax.rem(ta + i, n_ta), h, ta).start()
+            h_all[ta * hours_dev + h, gathered(b)] = staged[h, slices(b, ta)]
 
         return scores, powers, sums, end
 
@@ -343,11 +355,6 @@
 
     lax.fori_loop(0, hours_dev, spatial_hour, 0)
 
-    own_cot.wait()
-    others(n_ta, ta, lambda p: cot_copy(p, p).wait_recv())
-    for h in range(hours_dev):
-        others(n_ta, ta, lambda p, h=h: hidden_copy(p, h, p).wait_recv())
-
     def split(slab):
         return jnp.concatenate([slab[:, low : low + 8].reshape(BLOCK, WIDTH) for low in (0, 8)], axis=0)
 
@@ -355,7 +362,10 @@
         return jnp.concatenate([rows[low : low + BLOCK].reshape(hours, 8, WIDTH) for low in (0, BLOCK)], axis=1)
 
     def temporal_group(g, carry):
-        nodes = pl.ds(pl.multiple_of(g * GROUP, GROUP), GROUP)
+        own_cot(g).wait()
+        slabs_in(c_recv.at[g])
+        slabs_in(h_recv.at[g])
+        nodes = gathered(g)
         hidden = split(h_all[:, nodes].astype(F32))
         rows = normed(hidden, gt_ref[...][None])
         keys = dot(rows, wt_ref[:, WIDTH : 2 * WIDTH]).astype(BF16)
@@ -402,19 +412,19 @@
         staggered([(nodes_set, pair) for nodes_set in sets for pair in range(PAIRS)])
         cot = split(c_all[:, nodes].astype(F32)).astype(BF16)
         g_total[...] += dot(jnp.concatenate(attended, axis=1).astype(BF16), cot)
-        mixed = dot(jnp.concatenate([a.T for a in attended], axis=0).astype(BF16), wto_ref[...])
-        out_staged[:, nodes] = joined(hidden + mixed).astype(BF16)
+        att[g] = jnp.concatenate([a.T for a in attended], axis=0).astype(BF16)
+        return carry
+
+    def finished(g, carry):
+        nodes = gathered(g)
+        mixed = dot(att[g], wto_ref[...])
+        out_staged[:, nodes] = joined(split(h_all[:, nodes].astype(F32)) + mixed).astype(BF16)
         for i in range(1, n_ta):
             out_copy(g, lax.rem(ta + i, n_ta), ta).start()
+        own_out(g).start()
         return carry
 
     lax.fori_loop(0, groups, temporal_group, 0)
-    own_out = pltpu.make_async_copy(
-        out_staged.at[pl.ds(ta * hours_dev, hours_dev)],
-        out_ref.at[:, pl.ds(pl.multiple_of(ta * part, part), part)],
-        own_sem.at[1],
-    )
-    own_out.start()
 
     term = (g_total[...] * tokens ** (-0.5)).astype(BF16)
 
@@ -425,48 +435,66 @@
     pair_send[...] = terms_of(1 - core).astype(BF16)
     pair_copy.start()
     mine = terms_of(core)
+    finished(0, 0)
     pair_copy.wait_recv()
     g_send[...] = (mine + pair_recv[...].astype(F32)).astype(BF16)
     to_owners(lambda k: grad_copy(k, core * owners + k, af).start())
+    lax.fori_loop(1, groups, finished, 0)
+
+    def sent(g, carry):
+        slabs_out(c_send.at[g])
+        slabs_out(h_send.at[g])
+        return carry
+
+    lax.fori_loop(0, groups, sent, 0)
+    for h in range(hours_dev):
+        halo_right(h).wait_send()
+        halo_left(h).wait_send()
+
+    def count_waits(held_back, act):
+        @pl.when(holds)
+        def _():
+            act(held_back - 1)
+
+        @pl.when(jnp.logical_not(holds))
+        def _():
+            act(held_back)
 
     @pl.when(holds)
     def _():
         g_recv[af] = g_send[lax.rem(af, owners)]
-        others(n_af, af, lambda p: grad_copy(0, p, p).wait_recv())
+        arrived = g_recv.at[pl.ds(0, n_af - 1)]
+        to(partner, af, arrived, arrived, pair_sem.at[0], gr_sem.at[0]).wait_recv()
         t_send[...] = jnp.sum(g_recv[...].astype(F32), axis=0)
         others(n_ta, ta, lambda p: total_copy(p, ta // 2).start())
         t_recv[ta // 2] = t_send[...]
 
-    def holder_wait(n, carry):
-        source = 2 * n + af // owners
-
-        @pl.when(source != ta)
-        def _():
-            total_copy(source, n).wait_recv()
-
+    def out_waits(g, carry):
+        slabs_in(o_recv.at[g])
+        slabs_out(o_send.at[g])
+        own_out(g).wait()
         return carry
 
-    lax.fori_loop(0, n_ta // 2, holder_wait, 0)
+    pair_copy.wait_send()
+
+    def terms_sent(count):
+        sent_terms = g_send.at[pl.ds(0, count)]
+        to(partner, af, sent_terms, sent_terms, gs_sem.at[0], pair_sem.at[1]).wait_send()
+
+    count_waits(owners, terms_sent)
+    lax.fori_loop(0, groups, out_waits, 0)
+
+    def totals_in(count):
+        totals = t_recv.at[pl.ds(0, count)]
+        to(partner, af, totals, totals, pair_sem.at[0], tr_sem.at[0]).wait_recv()
+
+    count_waits(n_ta // 2, totals_in)
     grad_ref[...] = jnp.sum(t_recv[...], axis=0)[:OWNED]
-
-    def out_waits(g, carry):
-        others(n_ta, ta, lambda p: out_copy(g, p, p).wait_recv())
-        others(n_ta, ta, lambda p: out_copy(g, p, ta).wait_send())
-        return carry
-
-    lax.fori_loop(0, groups, out_waits, 0)
-    own_out.wait()
-    for h in range(hours_dev):
-        halo_right(h).wait_send()
-        halo_left(h).wait_send()
-        others(n_ta, ta, lambda p, h=h: hidden_copy(p, h, ta).wait_send())
-    others(n_ta, ta, lambda p: cot_copy(p, ta).wait_send())
-    pair_copy.wait_send()
-    to_owners(lambda k: grad_copy(k, core * owners + k, af).wait_send())
 
     @pl.when(holds)
     def _():
-        others(n_ta, ta, lambda p: total_copy(p, ta // 2).wait_send())
+        sent_rows = g_total.at[pl.ds(0, (n_ta - 1) * PADDED)]
+        to(partner, af, sent_rows, sent_rows, ts_sem.at[0], pair_sem.at[1]).wait_send()
 
 
 def shards(n_ta, n_af, features, ws, wso, wt, wto, gain_s, gain_t, neighbours, degrees, cotangent):
@@ -499,6 +527,7 @@
             pltpu.VMEM((hours_dev, nodes_dev, width), BF16),
             pltpu.VMEM((hours, part, width), BF16),
             pltpu.VMEM((hours, part, width), BF16),
+            pltpu.VMEM((groups, hours * GROUP, width), BF16),
             pltpu.VMEM((BLOCK, 2 * BLOCK), F32),
             pltpu.VMEM((n_af * PADDED, width), BF16),
             pltpu.VMEM((hours, part, width), BF16),
@@ -511,18 +540,18 @@
             pltpu.VMEM((n_ta // 2, PADDED, width), F32),
             dma((hours_dev, 2)),
             dma((hours_dev, 2)),
-            dma((n_ta,)),
-            dma((n_ta,)),
-            dma((hours_dev, n_ta)),
-            dma((hours_dev, n_ta)),
-            dma((groups, n_ta)),
-            dma((groups, n_ta)),
+            dma((groups,)),
+            dma((groups,)),
+            dma((groups,)),
+            dma((groups,)),
+            dma((groups,)),
+            dma((groups,)),
             dma((2,)),
-            dma((n_af // 2,)),
-            dma((n_af,)),
-            dma((n_ta,)),
-            dma((n_ta // 2,)),
-            dma((2,)),
+            dma((1,)),
+            dma((1,)),
+            dma((1,)),
+            dma((1,)),
+            dma((2, groups)),
             dma((9,)),
         ],
         compiler_params=pltpu.CompilerParams(

time: 58.9 us -> 53.5 us (0.908)
  Pallas kernels: 55.5 us -> 50.1 us
    pallas_call x1, Pallas kernels: 55.5 us -> 50.1 us  [shards(): pl.pallas_call(functools.partial(kernel, n_ta, n_af, hours * nodes_dev *...]
where the time goes in v5:
time: 53.5 us; the launch traced here: 53.4 us
  Pallas kernels  50.1 us (94%)
  local copies, waits for them, and re-layouts  2.71 us (5%)
  between operations  0.65 us (1%)
    pallas_call x1, Pallas kernels, shards(): pl.pallas_call(functools.partial(kernel, n_ta, n_af, hours * nodes_dev *...  50.1 us
    unnamed x4, local copies, waits for them, and re-layouts  2.71 us

profile of v5, /device:TPU:1, one launch (start us, length us, event | category | flops | bytes accessed | tf_op | source)
XLA Modules:
  0.0 53.4 jit_solution(4288825765751615086)
XLA Ops:
  0.6 50.1 %shard_map.113 = (bf16[2,512,384]{2,1,0:T(8,128)(2,1)}, f32[12,384]{1,0:T(8,128)}) custom-call(bf16[2,512,384]{2,1,0:T(8,128)(2,1)} %x_in.1, bf16[384,1152]{1,0:T(8,128)(2,1)} %ws_in.1, bf16[384,384]{1,0:T(8,128)(2,1)} %wso_in.1, bf16[384,1152]{1,0:T(8,128)(2,1)} %wt_in.1, bf16[384,384]{1,0:T(8,128)(2,1)} %wto_in.1, f32[384]{0:T(512)} %gs_in.1, f32[384]{0:T(512)} %gt_in.1, ...), custom_call_target="tpu_custom_call" | custom-call | tf_op jit(solution)/shard_map/pallas_call | solution.py:509
  50.7 0.0 copy-start
  50.7 2.1 %copy.14 = bf16[2,512,384]{2,1,0:T(8,128)(2,1)} copy(bf16[2,512,384]{2,1,0:T(8,128)(2,1)} %get-tuple-element.4) | data formatting | bytes 1572864
  52.8 0.0 copy-done
  52.8 0.6 %copy.15 = f32[12,384]{1,0:T(8,128)} copy(f32[12,384]{1,0:T(8,128)S(1)} %copy-done) | data formatting | bytes 36864
Async XLA Ops:
  50.7 2.1 %copy-start = (f32[12,384]{1,0:T(8,128)S(1)}, f32[12,384]{1,0:T(8,128)}, u32[]{:S(2)}) copy-start(f32[12,384]{1,0:T(8,128)} %get-tuple-element.5) | copy-start | bytes 55300

commit v6 on v5

--- a/solution.py
+++ b/solution.py
@@ -192,7 +192,11 @@
 
     owners = n_af // 2
     holds = af // owners == core
-    pair_copy = to(partner, af, pair_send, pair_recv, pair_sem.at[0], pair_sem.at[1])
+
+    def rows_of(core):
+        return pl.ds(pl.multiple_of(core * owners * OWNED, GROUP), owners * OWNED)
+
+    pair_copy = to(partner, af, pair_send.at[rows_of(1 - core)], pair_recv, pair_sem.at[0], pair_sem.at[1])
 
     def grad_copy(k, owner, slot):
         return to(ta, owner, g_send.at[k], g_recv.at[slot], gs_sem.at[0], gr_sem.at[0])
@@ -220,8 +224,15 @@
         lax.fori_loop(1, count, step, 0)
 
     barrier = pltpu.get_barrier_semaphore()
+    for p in (right, left):
+        pl.semaphore_signal(barrier, inc=1, device_id=(ta, p), device_id_type=MESH)
+
+    def greet(i, carry):
+        pl.semaphore_signal(barrier, inc=1, device_id=(ta, lax.rem(af + i, n_af)), device_id_type=MESH)
+        return carry
+
+    lax.fori_loop(2, n_af - 1, greet, 0)
     others(n_ta, ta, lambda p: pl.semaphore_signal(barrier, inc=1, device_id=(p, af), device_id_type=MESH))
-    others(n_af, af, lambda p: pl.semaphore_signal(barrier, inc=1, device_id=(ta, p), device_id_type=MESH))
 
     loads = [
         pltpu.make_async_copy(src, dst, in_sem.at[n])
@@ -426,18 +437,12 @@
 
     lax.fori_loop(0, groups, temporal_group, 0)
 
-    term = (g_total[...] * tokens ** (-0.5)).astype(BF16)
-
-    def terms_of(core):
-        rows = pl.ds(pl.multiple_of(core * owners * PADDED, PADDED), owners * PADDED)
-        return dot(picks[rows], term).reshape(owners, PADDED, WIDTH)
-
-    pair_send[...] = terms_of(1 - core).astype(BF16)
+    pair_send[...] = (g_total[...] * tokens ** (-0.5)).astype(BF16)
     pair_copy.start()
-    mine = terms_of(core)
     finished(0, 0)
     pair_copy.wait_recv()
-    g_send[...] = (mine + pair_recv[...].astype(F32)).astype(BF16)
+    both = (pair_send[rows_of(core)].astype(F32) + pair_recv[...].astype(F32)).astype(BF16)
+    g_send[...] = dot(picks[...], both).astype(BF16).reshape(owners, PADDED, WIDTH)
     to_owners(lambda k: grad_copy(k, core * owners + k, af).start())
     lax.fori_loop(1, groups, finished, 0)
 
@@ -529,11 +534,11 @@
             pltpu.VMEM((hours, part, width), BF16),
             pltpu.VMEM((groups, hours * GROUP, width), BF16),
             pltpu.VMEM((BLOCK, 2 * BLOCK), F32),
-            pltpu.VMEM((n_af * PADDED, width), BF16),
+            pltpu.VMEM((n_af // 2 * PADDED, n_af // 2 * OWNED), BF16),
             pltpu.VMEM((hours, part, width), BF16),
             pltpu.VMEM((width, width), F32),
-            pltpu.VMEM((n_af // 2, PADDED, width), BF16),
-            pltpu.VMEM((n_af // 2, PADDED, width), BF16),
+            pltpu.VMEM((width, width), BF16),
+            pltpu.VMEM((width // 2, width), BF16),
             pltpu.VMEM((n_af // 2, PADDED, width), BF16),
             pltpu.VMEM((n_af, PADDED, width), BF16),
             pltpu.VMEM((PADDED, width), F32),

time: 53.5 us -> 53.3 us (level)
  no operation moved by 1% of the time
where the time goes in v6:
time: 53.3 us; the launch traced here: 53.2 us
  Pallas kernels  49.8 us (93%)
  local copies, waits for them, and re-layouts  2.71 us (5%)
  between operations  0.65 us (1%)
    pallas_call x1, Pallas kernels, shards(): pl.pallas_call(functools.partial(kernel, n_ta, n_af, hours * nodes_dev *...  49.8 us
    unnamed x4, local copies, waits for them, and re-layouts  2.71 us

profile of v6, /device:TPU:1, one launch (start us, length us, event | category | flops | bytes accessed | tf_op | source)
XLA Modules:
  0.0 53.2 jit_solution(9411410485155636254)
XLA Ops:
  0.6 49.8 %shard_map.113 = (bf16[2,512,384]{2,1,0:T(8,128)(2,1)}, f32[12,384]{1,0:T(8,128)}) custom-call(bf16[2,512,384]{2,1,0:T(8,128)(2,1)} %x_in.1, bf16[384,1152]{1,0:T(8,128)(2,1)} %ws_in.1, bf16[384,384]{1,0:T(8,128)(2,1)} %wso_in.1, bf16[384,1152]{1,0:T(8,128)(2,1)} %wt_in.1, bf16[384,384]{1,0:T(8,128)(2,1)} %wto_in.1, f32[384]{0:T(512)} %gs_in.1, f32[384]{0:T(512)} %gt_in.1, ...), custom_call_target="tpu_custom_call" | custom-call | tf_op jit(solution)/shard_map/pallas_call | solution.py:514
  50.5 0.0 copy-start
  50.5 2.1 %copy.14 = bf16[2,512,384]{2,1,0:T(8,128)(2,1)} copy(bf16[2,512,384]{2,1,0:T(8,128)(2,1)} %get-tuple-element.4) | data formatting | bytes 1572864
  52.6 0.0 copy-done
  52.6 0.6 %copy.15 = f32[12,384]{1,0:T(8,128)} copy(f32[12,384]{1,0:T(8,128)S(1)} %copy-done) | data formatting | bytes 36864
Async XLA Ops:
  50.5 2.1 %copy-start = (f32[12,384]{1,0:T(8,128)S(1)}, f32[12,384]{1,0:T(8,128)}, u32[]{:S(2)}) copy-start(f32[12,384]{1,0:T(8,128)} %get-tuple-element.5) | copy-start | bytes 55300

commit v7 on v6

--- a/solution.py
+++ b/solution.py
@@ -166,9 +166,11 @@
         there = c_all.at[pl.ds(slot * hours_dev, hours_dev), gathered(b)]
         return to(peer, af, cot_ref.at[:, slices(b, peer)], there, c_send.at[b], c_recv.at[b])
 
-    def hidden_copy(b, peer, h, slot):
-        there = h_all.at[slot * hours_dev + h, gathered(b)]
-        return to(peer, af, staged.at[h, slices(b, peer)], there, h_send.at[b], h_recv.at[b])
+    def hidden_copy(two, peer, h, slot):
+        pair_of = pl.ds(2 * two, 2)
+        rows = pl.ds(pl.multiple_of(peer * GROUP, GROUP), GROUP)
+        there = h_all.at[slot * hours_dev + h, pair_of]
+        return to(peer, af, staged.at[h, pair_of, rows], there, h_send.at[two], h_recv.at[two])
 
     def out_copy(g, peer, slot):
         src = out_staged.at[pl.ds(peer * hours_dev, hours_dev), gathered(g)]
@@ -177,10 +179,12 @@
     slabs = (pl.ds(0, (n_ta - 1) * hours_dev), pl.ds(0, GROUP))
 
     def slabs_in(sem):
-        to(partner, af, c_all.at[slabs], h_all.at[slabs], own_sem.at[0, 0], sem).wait_recv()
+        to(partner, af, c_all.at[slabs], out_staged.at[slabs], own_sem.at[0, 0], sem).wait_recv()
+
+    twos = (pl.ds(0, (n_ta - 1) * hours_dev), pl.ds(0, 2))
 
     def slabs_out(sem):
-        to(partner, af, c_all.at[slabs], h_all.at[slabs], sem, own_sem.at[0, 0]).wait_send()
+        to(partner, af, c_all.at[slabs], out_staged.at[slabs], sem, own_sem.at[0, 0]).wait_send()
 
     def own_cot(b):
         there = c_all.at[pl.ds(ta * hours_dev, hours_dev), gathered(b)]
@@ -346,10 +350,11 @@
             rows = jnp.concatenate(attended, axis=0).T.astype(BF16)
             mixed = dot(rows, wso_ref[...])
             hidden = (x_ref[h, pl.ds(first, BLOCK)].astype(F32) + mixed).astype(BF16)
-            staged[h, pl.ds(first, BLOCK)] = hidden
-            for i in range(1, n_ta):
-                hidden_copy(b, lax.rem(ta + i, n_ta), h, ta).start()
-            h_all[ta * hours_dev + h, gathered(b)] = staged[h, slices(b, ta)]
+            staged[h, b] = hidden
+            h_all[ta * hours_dev + h, b] = staged[h, b, pl.ds(pl.multiple_of(ta * GROUP, GROUP), GROUP)]
+            if b % 2:
+                for i in range(1, n_ta):
+                    hidden_copy(b // 2, lax.rem(ta + i, n_ta), h, ta).start()
 
         return scores, powers, sums, end
 
@@ -372,12 +377,8 @@
     def joined(rows):
         return jnp.concatenate([rows[low : low + BLOCK].reshape(hours, 8, WIDTH) for low in (0, BLOCK)], axis=1)
 
-    def temporal_group(g, carry):
-        own_cot(g).wait()
-        slabs_in(c_recv.at[g])
-        slabs_in(h_recv.at[g])
-        nodes = gathered(g)
-        hidden = split(h_all[:, nodes].astype(F32))
+    def group_parts(g):
+        hidden = split(h_all[:, g].astype(F32))
         rows = normed(hidden, gt_ref[...][None])
         keys = dot(rows, wt_ref[:, WIDTH : 2 * WIDTH]).astype(BF16)
         queries = (dot_nt(wt_t[0], rows) * SCORE_SCALE).astype(BF16)
@@ -416,26 +417,39 @@
 
             def end():
                 attended.append(jnp.concatenate(column, axis=0))
+                if eight:
+                    att[g] = jnp.concatenate([a.T for a in attended], axis=0).astype(BF16)
 
             return scores, powers, sums, end
 
-        sets = [eight_nodes(eight) for eight in range(2)]
-        staggered([(nodes_set, pair) for nodes_set in sets for pair in range(PAIRS)])
-        cot = split(c_all[:, nodes].astype(F32)).astype(BF16)
-        g_total[...] += dot(jnp.concatenate(attended, axis=1).astype(BF16), cot)
-        att[g] = jnp.concatenate([a.T for a in attended], axis=0).astype(BF16)
+        return attended, [eight_nodes(eight) for eight in range(2)]
+
+    def temporal_two(two, carry):
+        to(partner, af, h_all.at[twos], h_all.at[twos], own_sem.at[0, 0], h_recv.at[two]).wait_recv()
+        cots = []
+        parts = []
+        for k in range(2):
+            g = 2 * two + k
+            own_cot(g).wait()
+            slabs_in(c_recv.at[g])
+            parts.append(group_parts(g))
+        staggered([(steps, pair) for _, sets in parts for steps in sets for pair in range(PAIRS)])
+        for k in range(2):
+            cots.append(split(c_all[:, gathered(2 * two + k)].astype(F32)).astype(BF16))
+        everything = jnp.concatenate([a for attended, _ in parts for a in attended], axis=1).astype(BF16)
+        g_total[...] += dot(everything, jnp.concatenate(cots, axis=0))
         return carry
 
     def finished(g, carry):
         nodes = gathered(g)
         mixed = dot(att[g], wto_ref[...])
-        out_staged[:, nodes] = joined(split(h_all[:, nodes].astype(F32)) + mixed).astype(BF16)
+        out_staged[:, nodes] = joined(split(h_all[:, g].astype(F32)) + mixed).astype(BF16)
         for i in range(1, n_ta):
             out_copy(g, lax.rem(ta + i, n_ta), ta).start()
         own_out(g).start()
         return carry
 
-    lax.fori_loop(0, groups, temporal_group, 0)
+    lax.fori_loop(0, groups // 2, temporal_two, 0)
 
     pair_send[...] = (g_total[...] * tokens ** (-0.5)).astype(BF16)
     pair_copy.start()
@@ -448,10 +462,11 @@
 
     def sent(g, carry):
         slabs_out(c_send.at[g])
-        slabs_out(h_send.at[g])
         return carry
 
     lax.fori_loop(0, groups, sent, 0)
+    for two in range(groups // 2):
+        to(partner, af, h_all.at[twos], h_all.at[twos], h_send.at[two], own_sem.at[0, 0]).wait_send()
     for h in range(hours_dev):
         halo_right(h).wait_send()
         halo_left(h).wait_send()
@@ -529,8 +544,8 @@
             pltpu.VMEM((hours_dev, HEADS, HEAD + PADDED, extended), BF16),
             pltpu.VMEM((2, width, width), BF16),
             pltpu.VMEM((2, width, width), BF16),
-            pltpu.VMEM((hours_dev, nodes_dev, width), BF16),
-            pltpu.VMEM((hours, part, width), BF16),
+            pltpu.VMEM((hours_dev, groups, BLOCK, width), BF16),
+            pltpu.VMEM((hours, groups, GROUP, width), BF16),
             pltpu.VMEM((hours, part, width), BF16),
             pltpu.VMEM((groups, hours * GROUP, width), BF16),
             pltpu.VMEM((BLOCK, 2 * BLOCK), F32),
@@ -547,8 +562,8 @@
             dma((hours_dev, 2)),
             dma((groups,)),
             dma((groups,)),
-            dma((groups,)),
-            dma((groups,)),
+            dma((groups // 2,)),
+            dma((groups // 2,)),
             dma((groups,)),
             dma((groups,)),
             dma((2,)),

time: 53.3 us -> 53.7 us (level)
  no operation moved by 1% of the time
where the time goes in v7:
time: 53.7 us; the launch traced here: 53.6 us
  Pallas kernels  50.3 us (94%)
  local copies, waits for them, and re-layouts  2.71 us (5%)
  between operations  0.65 us (1%)
    pallas_call x1, Pallas kernels, shards(): pl.pallas_call(functools.partial(kernel, n_ta, n_af, hours * nodes_dev *...  50.3 us
    unnamed x4, local copies, waits for them, and re-layouts  2.71 us

profile of v7, /device:TPU:1, one launch (start us, length us, event | category | flops | bytes accessed | tf_op | source)
XLA Modules:
  0.0 53.6 jit_solution(6859137331932449101)
XLA Ops:
  0.6 50.3 %shard_map.113 = (bf16[2,512,384]{2,1,0:T(8,128)(2,1)}, f32[12,384]{1,0:T(8,128)}) custom-call(bf16[2,512,384]{2,1,0:T(8,128)(2,1)} %x_in.1, bf16[384,1152]{1,0:T(8,128)(2,1)} %ws_in.1, bf16[384,384]{1,0:T(8,128)(2,1)} %wso_in.1, bf16[384,1152]{1,0:T(8,128)(2,1)} %wt_in.1, bf16[384,384]{1,0:T(8,128)(2,1)} %wto_in.1, f32[384]{0:T(512)} %gs_in.1, f32[384]{0:T(512)} %gt_in.1, ...), custom_call_target="tpu_custom_call" | custom-call | tf_op jit(solution)/shard_map/pallas_call | solution.py:529
  50.9 0.0 copy-start
  50.9 2.1 %copy.14 = bf16[2,512,384]{2,1,0:T(8,128)(2,1)} copy(bf16[2,512,384]{2,1,0:T(8,128)(2,1)} %get-tuple-element.4) | data formatting | bytes 1572864
  53.0 0.0 copy-done
  53.0 0.6 %copy.15 = f32[12,384]{1,0:T(8,128)} copy(f32[12,384]{1,0:T(8,128)S(1)} %copy-done) | data formatting | bytes 36864
Async XLA Ops:
  50.9 2.1 %copy-start = (f32[12,384]{1,0:T(8,128)S(1)}, f32[12,384]{1,0:T(8,128)}, u32[]{:S(2)}) copy-start(f32[12,384]{1,0:T(8,128)} %get-tuple-element.5) | copy-start | bytes 55300
